TPU v7x, 128 devices: a whole 4x4x4 slice. The times are simulated.
128 devices in a mesh: mesh: 32 (over y, z, core), comp: 4 (over x).
Axes of the slice: x: 4, y: 4, z: 4, core: 2. Of those that a mesh axis runs over, the one named last changes fastest.
Arguments:
- a_blocks: bfloat16 [6144, 64, 448], P(('mesh', 'comp')), may hold values from -0.25 to 0.25
- a_columns: int32 [6144, 7], P(('mesh', 'comp')), may hold values from 0 to 71, as said below
- p_blocks: bfloat16 [6144, 64, 192], P(('mesh', 'comp')), may hold values from -0.75 to 0.75
- p_columns: int32 [6144, 3], P(('mesh', 'comp')), may hold values from 0 to 3, all different within a row
- r_blocks: bfloat16 [6144, 64, 192], P(('mesh', 'comp')), may hold values from -0.75 to 0.75
- r_columns: int32 [6144, 3], P(('mesh', 'comp')), may hold values from 0 to 11, as said below
- sent_up: int32 [1536], P(('mesh', 'comp')), may hold values from 0 to 47, as said below
- sent_down: int32 [1536], P(('mesh', 'comp')), may hold values from 0 to 47, as said below
- vectors: bfloat16 [6144, 128], P(('mesh', 'comp')), may hold values from -2 to 2
- coarse_dest: int32 [512, 1], P(('mesh', 'comp')), may hold values from 0 to 3; in each aligned block of 4 rows (0 to 3, 4 to 7, ...) at most 2 rows name the same one
Outputs:
- coarse_matrix: bfloat16 [1024, 64, 1280], P(('mesh', 'comp'))
- coarse_vectors: bfloat16 [1024, 128], P(('mesh', 'comp'))
Inputs may be any that keep to these rules, and one draw needn't show every extreme that they name: `a_columns`: each fine row's first column is the row itself (its own local number). A column 48 + i exists only on devices with a device below along mesh, 60 + i only on devices with one above; every listed ghost of an existing neighbour is named by some row. `r_columns`: h is never toward a device missing along mesh. Local row numbers; the 12 entries of one device in sent_up and in sent_down are distinct, and no row is in both lists. `sent_down`: see sent_up. `coarse_dest`: at most 2 of the 4 coarse rows of one home go to one owner comp, and that many do in some home. `p_columns`: the 3 entries of a row are distinct.
All inputs are finite; a program needn't handle non-finite values.
Results may differ from a plain program's by a relative error of at most 0.0049.
Values may be sent and summed in bfloat16 or wider, within the bound.
No kernel may reach another device: no remote copies, remote signals or barrier semaphores. Data moves between devices by JAX's collectives and lax.ppermute only.
A program may use at most 128 MiB of HBM per device.

v0:
```python
import jax
import jax.numpy as jnp
from jax import lax
from jax.sharding import PartitionSpec as P


def passed_along(block, axis, distance):
    devices = range(lax.axis_size(axis))
    route = [(i - distance, i) for i in devices if i - distance in devices]
    return lax.ppermute(block, axis, route)


def densify(values, columns, coarse_count):
    count = values.shape[0]
    width = values.shape[1]
    blocks = values.reshape(count, width, columns.shape[1], width)
    onehot = (
        columns[:, :, None] == jnp.arange(coarse_count, dtype=jnp.int32)[None, None, :]
    ).astype(jnp.bfloat16)
    dense = jnp.einsum("rqs,rbqc->rbsc", onehot, blocks, preferred_element_type=jnp.float32)
    return dense.astype(jnp.bfloat16).reshape(count, width, coarse_count * width)


def widen(strip, offset, seg_width):
    return jnp.pad(strip, ((0, 0), (0, 0), ((1 - offset) * seg_width, (1 + offset) * seg_width)))


def on_device(
    a_blocks,
    a_columns,
    p_blocks,
    p_columns,
    r_blocks,
    r_columns,
    sent_up,
    sent_down,
    vectors,
    coarse_dest,
):
    fine_rows = a_blocks.shape[0]
    width = a_blocks.shape[1]
    a_count = a_columns.shape[1]
    r_count = r_columns.shape[1]
    ghosts = sent_up.shape[0]
    coarse_count = coarse_dest.shape[0]
    comp_count = lax.axis_size("comp")
    seg_width = coarse_count * width
    own_dense = densify(p_blocks, p_columns, coarse_count)
    from_lower = passed_along(own_dense[sent_up], "mesh", 1)
    from_upper = passed_along(own_dense[sent_down], "mesh", -1)
    p_table = jnp.concatenate([own_dense, from_lower, from_upper], 0)
    coarse_terms = jnp.zeros((3 * coarse_count, width, 3 * seg_width), jnp.float32)
    vec_terms = jnp.zeros((3 * coarse_count, 2, width), jnp.float32)
    gathered = p_table[a_columns]
    segment = jnp.where(a_columns < fine_rows, 1, jnp.where(a_columns < fine_rows + ghosts, 0, 2))
    chooser = (segment[:, :, None] == jnp.arange(3, dtype=jnp.int32)[None, None, :]).astype(
        jnp.float32
    )
    a_rows = a_blocks.reshape(fine_rows, width, a_count, width)
    product = jnp.einsum("fakb,fkbc->fkac", a_rows, gathered, preferred_element_type=jnp.float32)
    applied = jnp.einsum("fke,fkac->faec", chooser, product, precision=lax.Precision.HIGHEST)
    applied = applied.astype(jnp.bfloat16).reshape(fine_rows, width, 3 * seg_width)
    r_rows = r_blocks.reshape(fine_rows, width, r_count, width)
    vec_rows = vectors.reshape(fine_rows, 2, width)
    for j in range(r_count):
        targets = r_columns[0:fine_rows, j]
        contrib = jnp.einsum(
            "fab,fbx->fax", r_rows[:, :, j, :], applied, preferred_element_type=jnp.float32
        )
        coarse_terms = coarse_terms.at[targets].add(contrib)
        vec_part = jnp.einsum(
            "fab,ftb->fta", r_rows[:, :, j, :], vec_rows, preferred_element_type=jnp.float32
        )
        vec_terms = vec_terms.at[targets].add(vec_part)
    lower_piece = coarse_terms[:coarse_count]
    own_piece = coarse_terms[coarse_count : 2 * coarse_count]
    upper_piece = coarse_terms[2 * coarse_count :]
    from_above, above_vec = passed_along(
        (widen(lower_piece, -1, seg_width), vec_terms[:coarse_count]), "mesh", -1
    )
    from_below, below_vec = passed_along(
        (widen(upper_piece, 1, seg_width), vec_terms[2 * coarse_count :]), "mesh", 1
    )
    total = widen(own_piece, 0, seg_width) + from_above + from_below
    restricted = (vec_terms[coarse_count : 2 * coarse_count] + above_vec + below_vec).reshape(
        coarse_count, 2 * width
    )
    coarse_rows = total.astype(jnp.bfloat16)
    coarse_vec = restricted.astype(jnp.bfloat16)
    owner = coarse_dest[:, 0]
    onehot = (owner[:, None] == jnp.arange(comp_count, dtype=jnp.int32)[None, :]).astype(jnp.int32)
    ranking = jnp.sum((jnp.cumsum(onehot, 0) - onehot) * onehot, 1)
    capacity = max(2, coarse_count // 2)
    selector = (owner[None, None, :] == jnp.arange(comp_count, dtype=jnp.int32)[:, None, None]) & (
        ranking[None, None, :] == jnp.arange(capacity, dtype=jnp.int32)[None, :, None]
    )
    selector = selector.astype(jnp.bfloat16)
    outgoing = jnp.einsum(
        "dks,sax->dkax", selector, coarse_rows, preferred_element_type=jnp.float32
    ).astype(jnp.bfloat16)
    outgoing_vec = jnp.einsum(
        "dks,sx->dkx", selector, coarse_vec, preferred_element_type=jnp.float32
    ).astype(jnp.bfloat16)
    received, received_vec = (
        lax.all_to_all(outgoing, "comp", split_axis=0, concat_axis=0, tiled=True),
        lax.all_to_all(outgoing_vec, "comp", split_axis=0, concat_axis=0, tiled=True),
    )
    coarse_matrix = received.reshape(comp_count * capacity, width, 5 * seg_width)
    coarse_vectors = received_vec.reshape(comp_count * capacity, 2 * width)
    return (coarse_matrix, coarse_vectors)


def solution(mesh):
    placed = (
        P(("mesh", "comp"), None, None),
        P(("mesh", "comp"), None),
        P(("mesh", "comp"), None, None),
        P(("mesh", "comp"), None),
        P(("mesh", "comp"), None, None),
        P(("mesh", "comp"), None),
        P(("mesh", "comp")),
        P(("mesh", "comp")),
        P(("mesh", "comp"), None),
        P(("mesh", "comp"), None),
    )
    return jax.shard_map(
        on_device,
        mesh=mesh,
        in_specs=placed,
        out_specs=(P(("mesh", "comp"), None, None), P(("mesh", "comp"), None)),
        check_vma=False,
    )
```

profile of v0, /device:TPU:24, one launch (start us, length us, event | category | flops | bytes accessed | tf_op | source)
XLA Modules:
  0.0 239.1 jit_solution(13107797515800355402)
XLA Ops:
  0.6 2.9 %copy.42 = bf16[48,64,192]{1,2,0:T(8,128)(2,1)S(1)} copy(bf16[48,64,192]{2,1,0:T(8,128)(2,1)} %param.12) | data formatting | bytes 2359296 | tf_op args[2]
  3.5 3.6 %copy.43 = bf16[48,64,3,64]{3,2,1,0:T(4,128)(2,1)} copy(bf16[48,64,3,64]{1,3,2,0:T(8,128)(2,1)S(1)} %bitcast.76) | data formatting | bytes 2359296 | tf_op jit(solution)/shard_map/reshape | solution.py:16
  7.2 3.7 %convert_bitcast_fusion.1 = bf16[48,64,4,64]{3,2,1,0:T(4,128)(2,1)S(1)} fusion(bf16[48,64,3,64]{3,2,1,0:T(4,128)(2,1)} %copy.43, s32[48,3]{1,0:T(8,128)S(1)} %copy.41), kind=kOutput, calls=%fused_computation.17 | convolution fusion | flops 5505600 | bytes 2753088 | tf_op jit(solution)/shard_map/rqs,rbqc->rbsc/dot_general | solution.py:20
  10.9 3.0 %reshape.82 = bf16[48,64,256]{2,1,0:T(8,128)(2,1)} reshape(bf16[48,64,4,64]{3,2,1,0:T(4,128)(2,1)S(1)} %convert_bitcast_fusion.1) | data formatting | bytes 3145728 | tf_op jit(solution)/shard_map/reshape | solution.py:21
  17.9 2.7 %gather_fusion.1 = bf16[12,64,256]{2,1,0:T(8,128)(2,1)} fusion(bf16[48,64,256]{2,1,0:T(8,128)(2,1)} %reshape.82, s32[1024]{0:T(1024)S(1)} %pad_clamp_fusion.1), kind=kCustom, calls=%fused_computation.1 | custom fusion | bytes 786480 | tf_op jit(solution)/shard_map/gather | solution.py:50
  20.6 5.7 %collective-permute-start.1 = (bf16[12,64,256]{2,1,0:T(8,128)(2,1)}, bf16[12,64,256]{2,1,0:T(8,128)(2,1)S(1)}, u32[]{:S(2)}, u32[]{:S(2)}) collective-permute-start(bf16[12,64,256]{2,1,0:T(8,128)(2,1)} %gather_fusion.1), channel_id=1, source_target_pairs={{4,0},{8,4},{12,8},{16,12},{20,16},{24,20},{28,24},{32,28},{36,32}... | collective-permute-start | bytes 1179656 | tf_op jit(solution)/shard_map/ppermute | solution.py:10
  26.4 2.9 %copy.48 = bf16[48,64,192]{1,2,0:T(8,128)(2,1)S(1)} copy(bf16[48,64,192]{2,1,0:T(8,128)(2,1)} %param.14) | data formatting | bytes 2359296 | tf_op args[4]
  35.2 9.1 %reshape.83 = bf16[48,64,7,64]{3,2,1,0:T(8,128)(2,1)} reshape(bf16[48,64,448]{2,1,0:T(8,128)(2,1)} %param.10) | data formatting | bytes 5505024 | tf_op jit(solution)/shard_map/reshape | solution.py:59
  48.4 10.8 %gather_fusion.2 = bf16[336,64,256]{2,1,0:T(8,128)(2,1)} fusion(bf16[72,64,256]{2,1,0:T(8,128)(2,1)S(1)} %pad_maximum_fusion, s32[1024]{0:T(1024)S(1)} %pad_clamp_fusion), kind=kCustom, calls=%fused_computation.2 | custom fusion | bytes 22021440 | tf_op jit(solution)/shard_map/gather | solution.py:54
  59.2 16.3 %convolution_bitcast_fusion = f32[48,7,64,256]{3,2,1,0:T(8,128)} fusion(bf16[48,7,64,256]{3,2,1,0:T(8,128)(2,1)} %bitcast.69, bf16[48,64,7,64]{3,2,1,0:T(8,128)(2,1)} %reshape.83), kind=kOutput, calls=%fused_computation.11 | convolution fusion | flops 704643072 | bytes 35782656 | tf_op jit(solution)/shard_map/fakb,fkbc->fkac/dot_general | solution.py:60
  75.5 31.4 %convert_bitcast_fusion = bf16[48,64,3,256]{3,2,1,0:T(4,128)(2,1)} fusion(f32[48,7,64,256]{3,2,1,0:T(8,128)} %convolution_bitcast_fusion, s32[48,7]{1,0:T(8,128)S(1)} %copy-done.4), kind=kOutput, calls=%fused_computation.12 | convolution fusion | flops 200541168 | bytes 26740032 | tf_op jit(solution)/shard_map/fke,fkac->faec/dot_general | solution.py:61
  106.9 13.1 %reshape.84 = bf16[48,64,768]{2,1,0:T(8,128)(2,1)} reshape(bf16[48,64,3,256]{3,2,1,0:T(4,128)(2,1)} %convert_bitcast_fusion) | data formatting | bytes 9437184 | tf_op jit(solution)/shard_map/reshape | solution.py:62
  120.0 7.5 %convolution_bitcast_fusion.3 = f32[48,64,768]{2,1,0:T(8,128)} fusion(bf16[48,64,768]{2,1,0:T(8,128)(2,1)} %reshape.84, bf16[48,64,3,64]{1,3,2,0:T(8,128)(2,1)S(1)} %bitcast.73), kind=kOutput, calls=%fused_computation.16 | convolution fusion | flops 301989888 | bytes 14942208 | tf_op jit(solution)/shard_map/fab,fbx->fax/dot_general | solution.py:67
  127.6 5.1 %convolution_bitcast_fusion.2 = f32[48,64,768]{2,1,0:T(8,128)} fusion(bf16[48,64,768]{2,1,0:T(8,128)(2,1)S(1)} %copy-done, bf16[48,64,3,64]{1,3,2,0:T(8,128)(2,1)S(1)} %bitcast.74), kind=kOutput, calls=%fused_computation.15 | convolution fusion | flops 301989888 | bytes 14942208 | tf_op jit(solution)/shard_map/fab,fbx->fax/dot_general | solution.py:67
  132.6 5.1 %convolution_bitcast_fusion.1 = f32[48,64,768]{2,1,0:T(8,128)} fusion(bf16[48,64,768]{2,1,0:T(8,128)(2,1)S(1)} %copy-done, bf16[48,64,3,64]{1,3,2,0:T(8,128)(2,1)S(1)} %bitcast.75), kind=kOutput, calls=%fused_computation.14 | convolution fusion | flops 301989888 | bytes 14942208 | tf_op jit(solution)/shard_map/fab,fbx->fax/dot_general | solution.py:67
  138.0 15.0 %scatter_fusion = f32[12,64,768]{2,1,0:T(8,128)S(1)} fusion(f32[12,64,768]{2,1,0:T(8,128)S(1)} %broadcast_in_dim.20, s32[48]{0:T(128)S(1)} %copy-done.8, f32[48,64,768]{2,1,0:T(8,128)} %convolution_bitcast_fusion.3), kind=kCustom, calls=%fused_computation.3 | custom fusion | flops 2359296 | bytes 28311744 | tf_op jit(solution)/shard_map/scatter-add | solution.py:70
  153.0 14.8 %scatter_fusion.1 = f32[12,64,768]{2,1,0:T(8,128)S(1)} fusion(f32[12,64,768]{2,1,0:T(8,128)S(1)} %scatter_fusion, s32[48]{0:T(128)S(1)} %get-tuple-element.11, f32[48,64,768]{2,1,0:T(8,128)} %convolution_bitcast_fusion.2), kind=kCustom, calls=%fused_computation.4 | custom fusion | flops 2359296 | bytes 28311744 | tf_op jit(solution)/shard_map/scatter-add | solution.py:70
  167.8 14.8 %scatter_fusion.2 = f32[12,64,768]{2,1,0:T(8,128)S(1)} fusion(f32[12,64,768]{2,1,0:T(8,128)S(1)} %scatter_fusion.1, s32[48]{0:T(128)S(1)} %get-tuple-element.9, f32[48,64,768]{2,1,0:T(8,128)} %convolution_bitcast_fusion.1), kind=kCustom, calls=%fused_computation.5 | custom fusion | flops 2359296 | bytes 28311744 | tf_op jit(solution)/shard_map/scatter-add | solution.py:70
  184.0 2.4 %collective-permute-start.2 = (f32[4,64,1280]{2,1,0:T(8,128)}, f32[4,64,1280]{2,1,0:T(8,128)S(1)}, u32[]{:S(2)}, u32[]{:S(2)}) collective-permute-start(f32[4,64,1280]{2,1,0:T(8,128)} %pad.13), channel_id=1, source_target_pairs={{4,0},{8,4},{12,8},{16,12},{20,16},{24,20},{28,24},{32,28},{36,32}... | collective-permute-start | bytes 3932168 | tf_op jit(solution)/shard_map/ppermute | solution.py:10
  197.7 5.8 %collective-permute-start.4 = (f32[4,2,64]{2,1,0:T(2,128)S(1)}, f32[4,2,64]{2,1,0:T(2,128)S(1)}, u32[]{:S(2)}, u32[]{:S(2)}) collective-permute-start(f32[4,2,64]{2,1,0:T(2,128)S(1)} %get-tuple-element.5), channel_id=1, source_target_pairs={{4,0},{8,4},{12,8},{16,12},{20,16},{24,20},{28,24},{32,28},{36,32}... | collective-permute-start | bytes 6152 | tf_op jit(solution)/shard_map/ppermute | solution.py:10
  205.7 4.8 %collective-permute-done.5 = f32[4,2,64]{2,1,0:T(2,128)S(1)} collective-permute-done((f32[4,2,64]{2,1,0:T(2,128)S(1)}, f32[4,2,64]{2,1,0:T(2,128)S(1)}, u32[]{:S(2)}, u32[]{:S(2)}) %collective-permute-start.5) | collective-permute-done | bytes 2080 | tf_op jit(solution)/shard_map/ppermute | solution.py:10
  211.3 4.2 %all-to-all-start.1 = ((bf16[4,2,128]{2,1,0:T(2,128)(2,1)}), bf16[4,2,128]{2,1,0:T(2,128)(2,1)S(1)}, u32[]{:S(2)}, u32[]{:S(2)}) async-start(bf16[4,2,128]{2,1,0:T(2,128)(2,1)} %copy.54), calls=%async_computation.1 | async-start | bytes 4096 | tf_op jit(solution)/shard_map/all_to_all | solution.py:106
  220.7 3.5 %all-to-all-start = ((bf16[4,2,64,1280]{3,2,1,0:T(8,128)(2,1)}), bf16[4,2,64,1280]{3,2,1,0:T(8,128)(2,1)S(1)}, u32[]{:S(2)}, u32[]{:S(2)}) async-start(bf16[4,2,64,1280]{3,2,1,0:T(8,128)(2,1)} %copy.53), calls=%async_computation | async-start | bytes 2621440 | tf_op jit(solution)/shard_map/all_to_all | solution.py:105
  224.3 13.2 %all-to-all-done = bf16[4,2,64,1280]{3,2,1,0:T(8,128)(2,1)S(1)} async-done(((bf16[4,2,64,1280]{3,2,1,0:T(8,128)(2,1)}), bf16[4,2,64,1280]{3,2,1,0:T(8,128)(2,1)S(1)}, u32[]{:S(2)}, u32[]{:S(2)}) %all-to-all-start) | async-done | bytes 1310752 | tf_op jit(solution)/shard_map/all_to_all | solution.py:105
  (74 shorter events, 36.7 us)
Async XLA Ops:
  3.5 3.6 %copy-start.10 = (s32[48,3]{0,1:T(4,128)S(1)}, s32[48,3]{0,1:T(4,128)}, u32[]{:S(2)}) copy-start(s32[48,3]{0,1:T(4,128)} %param.13) | copy-start | bytes 1732
  10.9 3.0 %copy-start.11 = (s32[12]{0:T(128)S(1)}, s32[12]{0:T(128)}, u32[]{:S(2)}) copy-start(s32[12]{0:T(128)} %param.16) | copy-start | bytes 148
  10.9 6.9 %copy-start.12 = (s32[12]{0:T(128)S(1)}, s32[12]{0:T(128)}, u32[]{:S(2)}) copy-start(s32[12]{0:T(128)} %param.17) | copy-start | bytes 148
  10.9 15.5 %copy-start.9 = (s32[48,7]{0,1:T(8,128)S(1)}, s32[48,7]{0,1:T(8,128)}, u32[]{:S(2)}) copy-start(s32[48,7]{0,1:T(8,128)} %param.11) | copy-start | bytes 4036
  15.9 30.8 %collective-permute-start = (bf16[12,64,256]{2,1,0:T(8,128)(2,1)S(1)}, bf16[12,64,256]{2,1,0:T(8,128)(2,1)S(1)}, u32[]{:S(2)}, u32[]{:S(2)}) collective-permute-start(bf16[12,64,256]{2,1,0:T(8,128)(2,1)S(1)} %gather_fusion), channel_id=1, source_target_pairs={{0,4},{4,8},{8,12},{12,16},{16,20},{20,24},{24,28},{28,32},{32,36}... | collective-permute-start | bytes 1179656 | tf_op jit(solution)/shard_map/ppermute | solution.py:10
  20.6 26.1 %collective-permute-start.1 = (bf16[12,64,256]{2,1,0:T(8,128)(2,1)}, bf16[12,64,256]{2,1,0:T(8,128)(2,1)S(1)}, u32[]{:S(2)}, u32[]{:S(2)}) collective-permute-start(bf16[12,64,256]{2,1,0:T(8,128)(2,1)} %gather_fusion.1), channel_id=1, source_target_pairs={{4,0},{8,4},{12,8},{16,12},{20,16},{24,20},{28,24},{32,28},{36,32}... | collective-permute-start | bytes 1179656 | tf_op jit(solution)/shard_map/ppermute | solution.py:10
  29.3 15.8 %copy-start.1 = (bf16[48,64,192]{1,2,0:T(8,128)(2,1)}, bf16[48,64,192]{1,2,0:T(8,128)(2,1)S(1)}, u32[]{:S(2)}) copy-start(bf16[48,64,192]{1,2,0:T(8,128)(2,1)S(1)} %copy.48) | copy-start | bytes 3538948
  59.2 16.3 %copy-start.4 = (s32[48,7]{1,0:T(8,128)S(1)}, s32[48,7]{1,0:T(8,128)}, u32[]{:S(2)}) copy-start(s32[48,7]{1,0:T(8,128)} %copy.46) | copy-start | bytes 4036
  106.9 13.1 %copy-start.2 = (bf16[48,64,192]{1,2,0:T(8,128)(2,1)S(1)}, bf16[48,64,192]{1,2,0:T(8,128)(2,1)}, u32[]{:S(2)}) copy-start(bf16[48,64,192]{1,2,0:T(8,128)(2,1)} %copy-done.1) | copy-start | bytes 3538948
  120.0 7.5 %copy-start = (bf16[48,64,768]{2,1,0:T(8,128)(2,1)S(1)}, bf16[48,64,768]{2,1,0:T(8,128)(2,1)}, u32[]{:S(2)}) copy-start(bf16[48,64,768]{2,1,0:T(8,128)(2,1)} %reshape.84) | copy-start | bytes 14155780
  132.6 5.4 %copy-start.8 = (s32[48]{0:T(128)S(1)}, s32[48]{0:T(128)}, u32[]{:S(2)}) copy-start(s32[48]{0:T(128)} %get-tuple-element.10) | copy-start | bytes 580
  182.8 6.7 %copy-start.3 = (bf16[48,2,64]{2,1,0:T(2,128)(2,1)S(1)}, bf16[48,2,64]{2,1,0:T(2,128)(2,1)}, u32[]{:S(2)}) copy-start(bf16[48,2,64]{2,1,0:T(2,128)(2,1)} %reshape.87) | copy-start | bytes 36868
  182.8 8.2 %copy-start.5 = (f32[48,2,64]{2,1,0:T(2,128)S(1)}, f32[48,2,64]{2,1,0:T(2,128)}, u32[]{:S(2)}) copy-start(f32[48,2,64]{2,1,0:T(2,128)} %fusion.5) | copy-start | bytes 73732
  182.8 10.4 %copy-start.6 = (f32[48,2,64]{2,1,0:T(2,128)S(1)}, f32[48,2,64]{2,1,0:T(2,128)}, u32[]{:S(2)}) copy-start(f32[48,2,64]{2,1,0:T(2,128)} %fusion.6) | copy-start | bytes 73732
  182.8 22.6 %copy-start.7 = (s32[4,1]{0,1:T(1,128)S(1)}, s32[4,1]{0,1:T(1,128)}, u32[]{:S(2)}) copy-start(s32[4,1]{0,1:T(1,128)} %param.19) | copy-start | bytes 52
  184.0 31.5 %collective-permute-start.2 = (f32[4,64,1280]{2,1,0:T(8,128)}, f32[4,64,1280]{2,1,0:T(8,128)S(1)}, u32[]{:S(2)}, u32[]{:S(2)}) collective-permute-start(f32[4,64,1280]{2,1,0:T(8,128)} %pad.13), channel_id=1, source_target_pairs={{4,0},{8,4},{12,8},{16,12},{20,16},{24,20},{28,24},{32,28},{36,32}... | collective-permute-start | bytes 3932168 | tf_op jit(solution)/shard_map/ppermute | solution.py:10
  187.6 28.0 %collective-permute-start.3 = (f32[4,64,1280]{2,1,0:T(8,128)}, f32[4,64,1280]{2,1,0:T(8,128)}, u32[]{:S(2)}, u32[]{:S(2)}) collective-permute-start(f32[4,64,1280]{2,1,0:T(8,128)} %pad.14), channel_id=1, source_target_pairs={{0,4},{4,8},{8,12},{12,16},{16,20},{20,24},{24,28},{28,32},{32,36}... | collective-permute-start | bytes 3932168 | tf_op jit(solution)/shard_map/ppermute | solution.py:10
  197.7 8.0 %collective-permute-start.4 = (f32[4,2,64]{2,1,0:T(2,128)S(1)}, f32[4,2,64]{2,1,0:T(2,128)S(1)}, u32[]{:S(2)}, u32[]{:S(2)}) collective-permute-start(f32[4,2,64]{2,1,0:T(2,128)S(1)} %get-tuple-element.5), channel_id=1, source_target_pairs={{4,0},{8,4},{12,8},{16,12},{20,16},{24,20},{28,24},{32,28},{36,32}... | collective-permute-start | bytes 6152 | tf_op jit(solution)/shard_map/ppermute | solution.py:10
  203.5 7.0 %collective-permute-start.5 = (f32[4,2,64]{2,1,0:T(2,128)S(1)}, f32[4,2,64]{2,1,0:T(2,128)S(1)}, u32[]{:S(2)}, u32[]{:S(2)}) collective-permute-start(f32[4,2,64]{2,1,0:T(2,128)S(1)} %get-tuple-element.6), channel_id=1, source_target_pairs={{0,4},{4,8},{8,12},{12,16},{16,20},{20,24},{24,28},{28,32},{32,36}... | collective-permute-start | bytes 6152 | tf_op jit(solution)/shard_map/ppermute | solution.py:10
  211.3 9.4 %all-to-all-start.1 = ((bf16[4,2,128]{2,1,0:T(2,128)(2,1)}), bf16[4,2,128]{2,1,0:T(2,128)(2,1)S(1)}, u32[]{:S(2)}, u32[]{:S(2)}) async-start(bf16[4,2,128]{2,1,0:T(2,128)(2,1)} %copy.54), calls=%async_computation.1 | async-start | bytes 4096 | tf_op jit(solution)/shard_map/all_to_all | solution.py:106
  220.7 16.7 %all-to-all-start = ((bf16[4,2,64,1280]{3,2,1,0:T(8,128)(2,1)}), bf16[4,2,64,1280]{3,2,1,0:T(8,128)(2,1)S(1)}, u32[]{:S(2)}, u32[]{:S(2)}) async-start(bf16[4,2,64,1280]{3,2,1,0:T(8,128)(2,1)} %copy.53), calls=%async_computation | async-start | bytes 2621440 | tf_op jit(solution)/shard_map/all_to_all | solution.py:105
where the time goes:
time: 241 us; the launch traced here: 239 us
  matrix products  74.8 us (31%)
  local copies, waits for them, and re-layouts  60.1 us (25%)
  other arithmetic  56.2 us (23%)
  starting transfers between devices  27.4 us (11%)
  waiting for transfers between devices  19.6 us (8%)
    scatter-add x3, other arithmetic, on_device(): coarse_terms = coarse_terms.at[targets].add(contrib)  44.6 us
    dot_general x1, matrix products, on_device(): jnp.einsum('fke,fkac->faec', chooser, product, precision=lax.Precision.HI...  31.4 us
    ppermute x6, starting transfers between devices, passed_along(): return lax.ppermute(block, axis, route)  19.7 us
    dot_general x3, matrix products, on_device(): jnp.einsum('fab,fbx->fax', r_rows[:, :, j, :], applied, preferred_element...  17.7 us
    dot_general x1, matrix products, on_device(): jnp.einsum('fakb,fkbc->fkac', a_rows, gathered, preferred_element_type=jn...  16.3 us
    all_to_all x1, waiting for transfers between devices, on_device(): lax.all_to_all(outgoing, 'comp', split_axis=0, concat_axis=0, tiled=True)  13.2 us
    reshape x1, local copies, waits for them, and re-layouts, on_device(): applied.astype(jnp.bfloat16).reshape(fine_rows, width, 3 * seg_width)  13.1 us
    gather x1, local copies, waits for them, and re-layouts, on_device(): gathered = p_table[a_columns]  10.8 us
  transfers between devices with their start and end apart: 8, of which 3 were waited for; matrix products, arithmetic and copies ran while one was open for 15% of the time, Pallas kernels for 0%

commit v1 on v0

v1 whole, which is shorter than its diff:
```python
import functools

import jax
import jax.numpy as jnp
from jax import lax
from jax.experimental import pallas as pl
from jax.experimental.pallas import tpu as pltpu
from jax.sharding import PartitionSpec as P

BF = jnp.bfloat16
F32 = jnp.float32
MIB = 1 << 20


def params(mib=48):
    return pltpu.CompilerParams(vmem_limit_bytes=mib * MIB)


VM = pl.BlockSpec(memory_space=pltpu.VMEM)
SM = pl.BlockSpec(memory_space=pltpu.SMEM)
ANY = pl.BlockSpec(memory_space=pl.ANY)


def half_of_lane():
    return (lax.broadcasted_iota(jnp.int32, (16, 128), 1) >= 64).astype(jnp.int32)


def dense_row(x, cols, half, coarse):
    width = x.shape[0]
    tiles = []
    doubled = []
    for q in range(len(cols)):
        block = x[:, q * width : (q + 1) * width]
        doubled.append(jnp.concatenate([block, block], 1).reshape(width // 16, 16, 2 * width))
    for t in range(coarse // 2):
        total = None
        for q in range(len(cols)):
            mask = jnp.where(half == cols[q] - 2 * t, 1.0, 0.0).astype(BF)
            term = doubled[q] * mask[None]
            total = term if total is None else total + term
        tiles.append(total.reshape(width, 2 * width))
    return tiles


def send_kernel(pcol, up, down, par, p_ref, out_a, out_b, *, coarse):
    width = p_ref.shape[1]
    half = half_of_lane()
    even = par[0] == 0
    for i in range(up.shape[0]):
        for out, first, second in ((out_b, down, up), (out_a, up, down)):
            f = jnp.where(even, first[i], second[i])
            cols = [pcol[q, f] for q in range(pcol.shape[0])]
            tiles = dense_row(p_ref[f], cols, half, coarse)
            for t, tile in enumerate(tiles):
                out[i * width : (i + 1) * width, t * 128 : (t + 1) * 128] = tile


def own_kernel(
    acol, pcol, rcol, a_hbm, p_hbm, r_hbm, v_ref, ap_out, rd_out, a_v, p_v, r_v, table, sems, *, coarse
):
    rows, width = a_v.shape[0], a_v.shape[1]
    kas, krs = acol.shape[0], rcol.shape[0]
    copies = [
        pltpu.make_async_copy(p_hbm, p_v, sems.at[0]),
        pltpu.make_async_copy(r_hbm, r_v, sems.at[1]),
        pltpu.make_async_copy(a_hbm, a_v, sems.at[2]),
    ]
    for copy in copies:
        copy.start()
    half = half_of_lane()
    table[rows * width :, :] = jnp.zeros((width, coarse * width), BF)
    copies[0].wait()

    def densify(f, _):
        cols = [pcol[q, f] for q in range(pcol.shape[0])]
        at = pl.ds(pl.multiple_of(f * width, width), width)
        for t, tile in enumerate(dense_row(p_v[f], cols, half, coarse)):
            table[at, t * 128 : (t + 1) * 128] = tile
        return 0

    lax.fori_loop(0, rows, densify, 0, unroll=4)
    copies[1].wait()
    right = lax.broadcasted_iota(jnp.int32, (width, 128), 1) >= width
    for pair in range(rows // 2):
        lanes = slice(pair * 128, (pair + 1) * 128)
        one, other = r_v[2 * pair], r_v[2 * pair + 1]
        blocks, names = [], []
        for j in range(krs):
            cut = slice(j * width, (j + 1) * width)
            blocks.append(jnp.concatenate([one[:, cut], other[:, cut]], 1))
            names.append(jnp.where(right, rcol[j, 2 * pair + 1], rcol[j, 2 * pair]).astype(F32).astype(BF))
        for s in range(3 * coarse):
            total = None
            for block, name in zip(blocks, names):
                term = jnp.where(name == jnp.asarray(s, BF), block, jnp.zeros_like(block))
                total = term if total is None else total + term
            rd_out[s * width : (s + 1) * width, lanes] = total
    copies[2].wait()

    def apply(f, _):
        picked = []
        for k in range(kas):
            c = acol[k, f]
            c = jnp.where(c < rows, c, rows)
            picked.append(table[pl.ds(pl.multiple_of(c * width, width), width), :])
        strip = jnp.dot(a_v[f], jnp.concatenate(picked, 0), preferred_element_type=F32)
        ap_out[pl.ds(pl.multiple_of(f * width, width), width), :] = strip.astype(BF)
        return 0

    lax.fori_loop(0, rows, apply, 0, unroll=8)


def ghost_kernel(
    acol, par, got_a, got_b, a_hbm, rd_ref, ap_ref, v_ref, send_a, send_b, own, own_vec,
    a_v, table, strips, sems, *, coarse
):
    rows, width = a_v.shape[0], a_v.shape[1]
    kas = acol.shape[0]
    ghosts = got_a.shape[0] // width
    seg = coarse * width
    block = ghosts * width
    copy = pltpu.make_async_copy(a_hbm, a_v, sems.at[0])
    copy.start()
    odd = par[0]
    table[pl.ds(pl.multiple_of((1 - odd) * block, block), block), :] = got_a[...]
    table[pl.ds(pl.multiple_of(odd * block, block), block), :] = got_b[...]
    table[2 * block :, :] = jnp.zeros((width, seg), BF)
    strips[:, seg : 2 * seg] = ap_ref[...]

    flat = jnp.concatenate([v_ref[...].astype(F32), jnp.zeros((128 - rows, 2 * width), F32)], 0)
    turned = flat.T
    lane = lax.broadcasted_iota(jnp.int32, (width, 128), 1)
    both = jnp.where(lane < width, turned[:width], pltpu.roll(turned[width:], width, 1))
    at_lane = lane % width
    for f in range(rows):
        strips[f * width : (f + 1) * width, 3 * seg :] = jnp.where(at_lane == f, both, 0.0).astype(BF)
    copy.wait()

    def apply(f, _):
        at = pl.ds(pl.multiple_of(f * width, width), width)
        cols = [acol[k, f] - rows for k in range(kas)]
        for side in (0, 1):
            picked = []
            for k in range(kas):
                c = cols[k]
                inside = (c >= side * ghosts) & (c < (side + 1) * ghosts)
                c = jnp.where(inside, c, 2 * ghosts)
                picked.append(table[pl.ds(pl.multiple_of(c * width, width), width), :])
            strip = jnp.dot(a_v[f], jnp.concatenate(picked, 0), preferred_element_type=F32)
            strips[at, side * 2 * seg : (side * 2 + 1) * seg] = strip.astype(BF)
        return 0

    lax.fori_loop(0, rows, apply, 0, unroll=4)

    def restrict(start, out, out_vec, kind):
        r = rd_ref[pl.ds(pl.multiple_of(start, seg), seg), :]
        for e in range(3):
            lanes = slice(e * seg, (e + 1) * seg)
            out[0:seg, lanes] = jnp.dot(r, strips[:, lanes], preferred_element_type=F32).astype(kind)
        spread = jnp.dot(r, strips[:, 3 * seg :], preferred_element_type=F32)
        pieces = []
        for n in range(seg // 128):
            t = spread[n * 128 : (n + 1) * 128].T
            pieces.append(jnp.concatenate(
                [jnp.sum(t[i * width : (i + 1) * width], 0, keepdims=True) for i in range(2)], 0))
        vec = jnp.concatenate(pieces, 1)
        vec = jnp.concatenate([vec, jnp.zeros((14, seg), F32)], 0).astype(kind)
        if out_vec is None:
            out[seg : seg + 16, 0:seg] = vec
            out[seg : seg + 16, seg:] = jnp.zeros((16, 2 * seg), kind)
        else:
            out_vec[...] = vec

    restrict(seg * 2 * (1 - odd), send_a, None, BF)
    restrict(seg * 2 * odd, send_b, None, BF)
    restrict(seg, own, own_vec, F32)


def sum_kernel(dest, par, comp, got_a, got_b, own, own_vec, *outs, coarse):
    seg = own.shape[0]
    width = seg // coarse
    odd = par[0] == 1
    owners = [dest[0, s] for s in range(coarse)]
    ranks = []
    for s in range(coarse):
        rank = jnp.int32(0)
        for earlier in range(s):
            rank = rank + (owners[earlier] == owners[s]).astype(jnp.int32)
        ranks.append(rank)
    away = [lax.rem(owners[s] - comp[0] + 4, 4) for s in range(coarse)]
    low_vec = jnp.where(odd, got_a[seg : seg + 16, 0:seg].astype(F32), got_b[seg : seg + 16, 0:seg].astype(F32))
    high_vec = jnp.where(odd, got_b[seg : seg + 16, 0:seg].astype(F32), got_a[seg : seg + 16, 0:seg].astype(F32))
    vec = own_vec[...] + low_vec + high_vec
    lines = []
    for s in range(coarse):
        lines.append(jnp.concatenate(
            [vec[0:1, s * width : (s + 1) * width], vec[1:2, s * width : (s + 1) * width]], 1))
    row = lax.broadcasted_iota(jnp.int32, (16, 128), 0)
    for distance, out in enumerate(outs):
        block = jnp.zeros((16, 128), F32)
        for s in range(coarse):
            hit = jnp.where(away[s] == distance, ranks[s], -1)
            block = block + jnp.where(row == hit, lines[s], 0.0)
        out[2 * width :, 0:128] = block.astype(BF)
        out[2 * width :, 128:] = jnp.zeros((16, 5 * seg - 128), BF)
        for k in range(2):
            source = jnp.int32(-1)
            for s in range(coarse):
                source = jnp.where((away[s] == distance) & (ranks[s] == k), s, source)
            into = slice(k * width, (k + 1) * width)

            def fill(below, above, out=out, into=into, source=source):
                at = pl.ds(pl.multiple_of(jnp.maximum(source, 0) * width, width), width)
                for u in range(5):
                    total = None
                    for ref, first in ((own, 1), (below, 0), (above, 2)):
                        e = u - first
                        if 0 <= e < 3:
                            term = ref[at, e * seg : (e + 1) * seg].astype(F32)
                            total = term if total is None else total + term
                    out[into, u * seg : (u + 1) * seg] = total.astype(BF)

            @pl.when((source >= 0) & odd)
            def _():
                fill(got_a, got_b)

            @pl.when((source >= 0) & jnp.logical_not(odd))
            def _():
                fill(got_b, got_a)

            @pl.when(source < 0)
            def _():
                out[into, :] = jnp.zeros((width, 5 * seg), BF)


def gather_kernel(comp, *refs):
    parts, matrix, vectors = refs[:4], refs[4], refs[5]
    width = matrix.shape[1]
    row = lax.broadcasted_iota(jnp.int32, (8, 128), 0)
    total = jnp.zeros((8, 128), F32)
    for distance, part in enumerate(parts):
        source = lax.rem(comp[0] - distance + 4, 4)
        for k in range(2):
            matrix[source * 2 + k] = part[k * width : (k + 1) * width, :]
            line = part[2 * width :, 0:128].astype(F32)[k : k + 1]
            total = total + jnp.where(row == source * 2 + k, line, 0.0)
    vectors[...] = total.astype(BF)


def exchange(block_a, block_b):
    n = lax.axis_size("mesh")
    within = [(i, i ^ 1) for i in range(n)]
    across = [(i, i + 1 if i % 2 else i - 1) for i in range(1, n - 1)]
    got_b = lax.ppermute(block_b, "mesh", across)
    got_a = lax.ppermute(block_a, "mesh", within)
    return got_a, got_b


def on_device(a_blocks, a_columns, p_blocks, p_columns, r_blocks, r_columns, sent_up, sent_down, vectors, coarse_dest):
    rows, width = a_blocks.shape[0], a_blocks.shape[1]
    ghosts = sent_up.shape[0]
    coarse = coarse_dest.shape[0]
    seg = coarse * width
    acol, pcol, rcol, dest = a_columns.T, p_columns.T, r_columns.T, coarse_dest.T
    par = (lax.axis_index("mesh") % 2).astype(jnp.int32).reshape(1)
    comp = lax.axis_index("comp").astype(jnp.int32).reshape(1)
    shape = jax.ShapeDtypeStruct
    out_a, out_b = pl.pallas_call(
        functools.partial(send_kernel, coarse=coarse),
        out_shape=[shape((ghosts * width, seg), BF)] * 2,
        in_specs=[SM, SM, SM, SM, VM],
        out_specs=[VM, VM],
        compiler_params=params(),
        name="send_rows",
    )(pcol, sent_up, sent_down, par, p_blocks)
    got_a, got_b = exchange(out_a, out_b)
    strips, r_dense = pl.pallas_call(
        functools.partial(own_kernel, coarse=coarse),
        out_shape=[shape((rows * width, seg), BF), shape((3 * seg, rows * width), BF)],
        in_specs=[SM, SM, SM, ANY, ANY, ANY, VM],
        out_specs=[VM, VM],
        scratch_shapes=[
            pltpu.VMEM(a_blocks.shape, BF),
            pltpu.VMEM(p_blocks.shape, BF),
            pltpu.VMEM(r_blocks.shape, BF),
            pltpu.VMEM(((rows + 1) * width, seg), BF),
            pltpu.SemaphoreType.DMA((3,)),
        ],
        compiler_params=params(),
        cost_estimate=pl.CostEstimate(flops=4 * 10**9, bytes_accessed=20 * 10**6, transcendentals=0),
        name="own_columns",
    )(acol, pcol, rcol, a_blocks, p_blocks, r_blocks, vectors)
    send_a, send_b, own, own_vec = pl.pallas_call(
        functools.partial(ghost_kernel, coarse=coarse),
        out_shape=[shape((seg + 16, 3 * seg), BF)] * 2 + [shape((seg, 3 * seg), F32), shape((16, seg), F32)],
        in_specs=[SM, SM, VM, VM, ANY, VM, VM, VM],
        out_specs=[VM] * 4,
        scratch_shapes=[
            pltpu.VMEM(a_blocks.shape, BF),
            pltpu.VMEM(((2 * ghosts + 1) * width, seg), BF),
            pltpu.VMEM((rows * width, 3 * seg + 128), BF),
            pltpu.SemaphoreType.DMA((1,)),
        ],
        compiler_params=params(),
        name="ghost_columns",
    )(acol, par, got_a, got_b, a_blocks, r_dense, strips, vectors)
    from_a, from_b = exchange(send_a, send_b)
    outs = pl.pallas_call(
        functools.partial(sum_kernel, coarse=coarse),
        out_shape=[shape((2 * width + 16, 5 * seg), BF)] * 4,
        in_specs=[SM, SM, SM, VM, VM, VM, VM],
        out_specs=[VM] * 4,
        compiler_params=params(),
        name="sum_rows",
    )(dest, par, comp, from_a, from_b, own, own_vec)
    parts = [outs[0]]
    turned = {}
    for distance in (2, 1, 3):
        turned[distance] = lax.ppermute(outs[distance], "comp", [(i, (i + distance) % 4) for i in range(4)])
    return pl.pallas_call(
        gather_kernel,
        out_shape=[shape((8, width, 5 * seg), BF), shape((8, 2 * width), BF)],
        in_specs=[SM] + [VM] * 4,
        out_specs=[VM, VM],
        compiler_params=params(),
        name="into_slots",
    )(comp, outs[0], turned[1], turned[2], turned[3])


def solution(mesh):
    placed = (
        P(("mesh", "comp"), None, None),
        P(("mesh", "comp"), None),
        P(("mesh", "comp"), None, None),
        P(("mesh", "comp"), None),
        P(("mesh", "comp"), None, None),
        P(("mesh", "comp"), None),
        P(("mesh", "comp")),
        P(("mesh", "comp")),
        P(("mesh", "comp"), None),
        P(("mesh", "comp"), None),
    )
    return jax.shard_map(
        on_device,
        mesh=mesh,
        in_specs=placed,
        out_specs=(P(("mesh", "comp"), None, None), P(("mesh", "comp"), None)),
        check_vma=False,
    )
```

time: 241 us -> 69.6 us (0.29)
  matrix products: 74.8 us -> 0 us
  other arithmetic: 56.2 us -> 0 us
  local copies, waits for them, and re-layouts: 60.1 us -> 4.82 us
  Pallas kernels: 0 us -> 26.5 us
  starting transfers between devices: 27.4 us -> 14.5 us
  waiting for transfers between devices: 19.6 us -> 22.7 us
    dot_general x11 -> x0, matrix products: 74.8 us -> none  [the longest x1 31.4 us: on_device(): jnp.einsum('fke,fkac->faec', chooser, product, precision=lax.Precision.HI...]
    scatter-add x6 -> x0, other arithmetic: 51.3 us -> none  [the longest x3 44.6 us: on_device(): coarse_terms = coarse_terms.at[targets].add(contrib)]
    reshape x5 -> x0, local copies, waits for them, and re-layouts: 30.3 us -> none  [the longest x1 13.1 us: on_device(): applied.astype(jnp.bfloat16).reshape(fine_rows, width, 3 * seg_width)]
    pallas_call x0 -> x5, Pallas kernels: none -> 26.5 us  [the longest x1 14.6 us: on_device(): pl.pallas_call(functools.partial(ghost_kernel, coarse=coarse), out_shape=...]
    ppermute x6 -> x7, waiting for transfers between devices: 4.8 us -> 22.7 us  [the longest x3 13.6 us: on_device(): lax.ppermute(outs[distance], 'comp', [(i, (i + distance) % 4) for i in ra...]
    gather x3 -> x0, local copies, waits for them, and re-layouts: 15.6 us -> none  [the longest x1 10.8 us: on_device(): gathered = p_table[a_columns]]
    all_to_all x2 -> x0, waiting for transfers between devices: 14.8 us -> none  [the longest x1 13.2 us: on_device(): lax.all_to_all(outgoing, 'comp', split_axis=0, concat_axis=0, tiled=True)]
    all_to_all x2 -> x0, starting transfers between devices: 7.74 us -> none  [the longest x1 4.19 us: on_device(): lax.all_to_all(outgoing_vec, 'comp', split_axis=0, concat_axis=0, tiled=T...]
  transfers between devices with their start and end apart: 8 -> 7, of which waited for: 3 -> 3; matrix products, arithmetic and copies ran while one was open for 15% -> 0% of each run, Pallas kernels for 0% -> 13%
where the time goes in v1:
time: 69.6 us; the launch traced here: 69.3 us
  Pallas kernels  26.5 us (38%)
  waiting for transfers between devices  22.7 us (33%)
  starting transfers between devices  14.5 us (21%)
  local copies, waits for them, and re-layouts  4.82 us (7%)
  between operations  0.82 us (1%)
    pallas_call x1, Pallas kernels, on_device(): pl.pallas_call(functools.partial(ghost_kernel, coarse=coarse), out_shape=...  14.6 us
    ppermute x3, waiting for transfers between devices, on_device(): lax.ppermute(outs[distance], 'comp', [(i, (i + distance) % 4) for i in ra...  13.6 us
    ppermute x2, waiting for transfers between devices, exchange(): got_b = lax.ppermute(block_b, 'mesh', across)  9.05 us
    pallas_call x1, Pallas kernels, on_device(): pl.pallas_call(functools.partial(own_kernel, coarse=coarse), out_shape=[s...  8.9 us
    ppermute x2, starting transfers between devices, exchange(): got_b = lax.ppermute(block_b, 'mesh', across)  8.61 us
    ppermute x3, starting transfers between devices, on_device(): lax.ppermute(outs[distance], 'comp', [(i, (i + distance) % 4) for i in ra...  5.73 us
    unnamed x20, local copies, waits for them, and re-layouts  4.82 us
  transfers between devices with their start and end apart: 7, of which 3 were waited for; matrix products, arithmetic and copies ran while one was open for 0% of the time, Pallas kernels for 13%

profile of v1, /device:TPU:24, one launch (start us, length us, event | category | flops | bytes accessed | tf_op | source)
XLA Modules:
  0.0 69.3 jit_solution(12759987163391047403)
XLA Ops:
  0.7 1.4 %copy-done = bf16[48,64,192]{2,1,0:T(8,128)(2,1)S(1)} copy-done((bf16[48,64,192]{2,1,0:T(8,128)(2,1)S(1)}, bf16[48,64,192]{2,1,0:T(8,128)(2,1)}, u32[]{:S(2)}) %copy-start) | copy-done | bytes 1179672
  2.1 0.7 copy-done.4
  2.8 0.7 copy-done.5
  3.4 0.7 copy-done.6
  4.1 0.9 %send_rows.1 = (bf16[768,256]{1,0:T(8,128)(2,1)S(1)}, bf16[768,256]{1,0:T(8,128)(2,1)S(1)}) custom-call(s32[3,48]{1,0:T(4,128)S(1)} %bitcast.8, s32[12]{0:T(128)S(1)} %copy-done.5, s32[12]{0:T(128)S(1)} %copy-done.6, s32[1]{0:T(128)} %bitcast.2.par, bf16[48,64,192]{2,1,0:T(8,128)(2,1)S(1)} %copy-done), custom_call_target="tpu_custom_call" | custom-call | tf_op jit(solution)/shard_map/send_rows/pallas_call | solution.py:268
  5.0 0.1 collective-permute-start
  5.1 6.2 %collective-permute-start.1 = (bf16[768,256]{1,0:T(8,128)(2,1)S(1)}, bf16[768,256]{1,0:T(8,128)(2,1)S(1)}, u32[]{:S(2)}, u32[]{:S(2)}) collective-permute-start(bf16[768,256]{1,0:T(8,128)(2,1)S(1)} %get-tuple-element.15), channel_id=1, source_target_pairs={{4,8},{8,4},{12,16},{16,12},{20,24},{24,20},{28,32},{32,28},{36,40... | collective-permute-start | bytes 1179656 | tf_op jit(solution)/shard_map/ppermute | solution.py:254
  11.4 0.0 copy-start.8
  11.4 1.4 %copy-done.8 = bf16[48,64,192]{2,1,0:T(8,128)(2,1)S(1)} copy-done((bf16[48,64,192]{2,1,0:T(8,128)(2,1)S(1)}, bf16[48,64,192]{2,1,0:T(8,128)(2,1)}, u32[]{:S(2)}) %copy-start.8) | copy-done | bytes 1179672
  12.8 8.9 %own_columns.1 = (bf16[3072,256]{1,0:T(8,128)(2,1)S(1)}, bf16[768,3072]{1,0:T(8,128)(2,1)}) custom-call(s32[7,48]{1,0:T(8,128)S(1)} %bitcast.6, s32[3,48]{1,0:T(4,128)S(1)} %bitcast.9, s32[3,48]{1,0:T(4,128)S(1)} %bitcast.11, bf16[48,64,448]{2,1,0:T(8,128)(2,1)} %a_hbm.3, bf16[48,64,192]{2,1,0:T(8,128)(2,1)S(1)} %copy-done.1, ...), custom_call_target="tpu_custom_call" | custom-call | flops 4000000000 | bytes 20000000 | tf_op jit(solution)/shard_map/own_columns/pallas_call | solution.py:277
  21.7 0.0 collective-permute-done.got_a
  21.7 0.0 collective-permute-done.1.got_b
  21.7 0.0 copy-start.7
  21.7 14.6 %ghost_columns.1 = (bf16[272,768]{1,0:T(8,128)(2,1)S(1)}, bf16[272,768]{1,0:T(8,128)(2,1)S(1)}, f32[256,768]{1,0:T(8,128)S(1)}, f32[16,256]{1,0:T(8,128)S(1)}) custom-call(s32[7,48]{1,0:T(8,128)S(1)} %bitcast.7, s32[1]{0:T(128)} %bitcast.2.par, bf16[768,256]{1,0:T(8,128)(2,1)S(1)} %collective-permute-done.got_a, ...), custom_call_target="tpu_custom_call" | custom-call | tf_op jit(solution)/shard_map/ghost_columns/pallas_call | solution.py:293
  36.4 0.1 collective-permute-start.2
  36.5 2.4 %collective-permute-start.3 = (bf16[272,768]{1,0:T(8,128)(2,1)S(1)}, bf16[272,768]{1,0:T(8,128)(2,1)S(1)}, u32[]{:S(2)}, u32[]{:S(2)}) collective-permute-start(bf16[272,768]{1,0:T(8,128)(2,1)S(1)} %get-tuple-element.19), channel_id=1, source_target_pairs={{4,8},{8,4},{12,16},{16,12},{20,24},{24,20},{28,32},{32,28},{36,40... | collective-permute-start | bytes 1253384 | tf_op jit(solution)/shard_map/ppermute | solution.py:254
  38.9 9.1 %collective-permute-done.3.got_b = bf16[272,768]{1,0:T(8,128)(2,1)S(1)} collective-permute-done((bf16[272,768]{1,0:T(8,128)(2,1)S(1)}, bf16[272,768]{1,0:T(8,128)(2,1)S(1)}, u32[]{:S(2)}, u32[]{:S(2)}) %collective-permute-start.3) | collective-permute-done | bytes 417824 | tf_op jit(solution)/shard_map/ppermute | solution.py:254
  47.9 0.9 %sum_rows.1 = (bf16[144,1280]{1,0:T(8,128)(2,1)S(1)}, bf16[144,1280]{1,0:T(8,128)(2,1)S(1)}, bf16[144,1280]{1,0:T(8,128)(2,1)S(1)}, bf16[144,1280]{1,0:T(8,128)(2,1)S(1)}) custom-call(s32[1,4]{1,0:T(1,128)S(1)} %bitcast.10, s32[1]{0:T(128)} %bitcast.2.par, s32[1]{0:T(128)} %bitcast.comp, bf16[272,768]{1,0:T(8,128)(2,1)S(1)} %collective-permute-done.2.got_a, ...), custom_call_target="tpu_custom_call" | custom-call | tf_op jit(solution)/shard_map/sum_rows/pallas_call | solution.py:308
  48.9 1.6 %collective-permute-start.4 = (bf16[144,1280]{1,0:T(8,128)(2,1)S(1)}, bf16[144,1280]{1,0:T(8,128)(2,1)S(1)}, u32[]{:S(2)}, u32[]{:S(2)}) collective-permute-start(bf16[144,1280]{1,0:T(8,128)(2,1)S(1)} %get-tuple-element.23), channel_id=1, source_target_pairs={{0,1},{1,2},{2,3},{3,0},{4,5},{5,6},{6,7},{7,4},{8,9},{9,10},{10,1... | collective-permute-start | bytes 1105928 | tf_op jit(solution)/shard_map/ppermute | solution.py:319
  50.4 2.7 %collective-permute-start.5 = (bf16[144,1280]{1,0:T(8,128)(2,1)S(1)}, bf16[144,1280]{1,0:T(8,128)(2,1)S(1)}, u32[]{:S(2)}, u32[]{:S(2)}) collective-permute-start(bf16[144,1280]{1,0:T(8,128)(2,1)S(1)} %get-tuple-element.24), channel_id=1, source_target_pairs={{0,2},{1,3},{2,0},{3,1},{4,6},{5,7},{6,4},{7,5},{8,10},{9,11},{10,... | collective-permute-start | bytes 1105928 | tf_op jit(solution)/shard_map/ppermute | solution.py:319
  53.1 1.4 %collective-permute-start.6 = (bf16[144,1280]{1,0:T(8,128)(2,1)S(1)}, bf16[144,1280]{1,0:T(8,128)(2,1)S(1)}, u32[]{:S(2)}, u32[]{:S(2)}) collective-permute-start(bf16[144,1280]{1,0:T(8,128)(2,1)S(1)} %get-tuple-element.25), channel_id=1, source_target_pairs={{0,3},{1,0},{2,1},{3,2},{4,7},{5,4},{6,5},{7,6},{8,11},{9,8},{10,9... | collective-permute-start | bytes 1105928 | tf_op jit(solution)/shard_map/ppermute | solution.py:319
  54.6 6.1 %collective-permute-done.4.refs_1_ = bf16[144,1280]{1,0:T(8,128)(2,1)S(1)} collective-permute-done((bf16[144,1280]{1,0:T(8,128)(2,1)S(1)}, bf16[144,1280]{1,0:T(8,128)(2,1)S(1)}, u32[]{:S(2)}, u32[]{:S(2)}) %collective-permute-start.4) | collective-permute-done | bytes 368672 | tf_op jit(solution)/shard_map/ppermute | solution.py:319
  60.7 7.5 %collective-permute-done.5.refs_2_ = bf16[144,1280]{1,0:T(8,128)(2,1)S(1)} collective-permute-done((bf16[144,1280]{1,0:T(8,128)(2,1)S(1)}, bf16[144,1280]{1,0:T(8,128)(2,1)S(1)}, u32[]{:S(2)}, u32[]{:S(2)}) %collective-permute-start.5) | collective-permute-done | bytes 368672 | tf_op jit(solution)/shard_map/ppermute | solution.py:319
  68.2 1.1 %into_slots.1 = (bf16[8,64,1280]{2,1,0:T(8,128)(2,1)}, bf16[8,128]{1,0:T(8,128)(2,1)}) custom-call(s32[1]{0:T(128)} %bitcast.comp, bf16[144,1280]{1,0:T(8,128)(2,1)S(1)} %get-tuple-element.22.refs_0_, bf16[144,1280]{1,0:T(8,128)(2,1)S(1)} %collective-permute-done.4.refs_1_, bf16[144,1280]{1,0:T(8,128)(2,1)S(1)} %collective-permute-done.5.refs_2_, ...), custom_call_target="tpu_custom_call" | custom-call | tf_op jit(solution)/shard_map/into_slots/pallas_call | solution.py:320
  (15 shorter events, 0.0 us)
Async XLA Ops:
  0.6 10.7 %copy-start.2 = (bf16[48,128]{1,0:T(8,128)(2,1)S(1)}, bf16[48,128]{1,0:T(8,128)(2,1)}, u32[]{:S(2)}) copy-start(bf16[48,128]{1,0:T(8,128)(2,1)} %v_ref.3) | copy-start | bytes 36868
  0.6 10.7 %copy-start.9 = (s32[48,3]{0,1:T(4,128)S(1)}, s32[48,3]{0,1:T(4,128)}, u32[]{:S(2)}) copy-start(s32[48,3]{0,1:T(4,128)} %param.15) | copy-start | bytes 1732
  0.7 10.7 %copy-start.3 = (s32[48,7]{0,1:T(8,128)S(1)}, s32[48,7]{0,1:T(8,128)}, u32[]{:S(2)}) copy-start(s32[48,7]{0,1:T(8,128)} %param.11) | copy-start | bytes 4036
  0.7 1.4 %copy-start = (bf16[48,64,192]{2,1,0:T(8,128)(2,1)S(1)}, bf16[48,64,192]{2,1,0:T(8,128)(2,1)}, u32[]{:S(2)}) copy-start(bf16[48,64,192]{2,1,0:T(8,128)(2,1)} %p_hbm.1) | copy-start | bytes 3538948
  2.1 0.7 copy-start.4
  2.8 0.7 copy-start.5
  3.4 0.7 copy-start.6
  4.1 7.3 %copy-start.1 = (bf16[48,64,192]{2,1,0:T(8,128)(2,1)S(1)}, bf16[48,64,192]{2,1,0:T(8,128)(2,1)}, u32[]{:S(2)}) copy-start(bf16[48,64,192]{2,1,0:T(8,128)(2,1)} %p_hbm.1) | copy-start | bytes 3538948
  5.0 16.7 %collective-permute-start = (bf16[768,256]{1,0:T(8,128)(2,1)S(1)}, bf16[768,256]{1,0:T(8,128)(2,1)S(1)}, u32[]{:S(2)}, u32[]{:S(2)}) collective-permute-start(bf16[768,256]{1,0:T(8,128)(2,1)S(1)} %get-tuple-element.14), channel_id=1, source_target_pairs={{0,4},{4,0},{8,12},{12,8},{16,20},{20,16},{24,28},{28,24},{32,36},... | collective-permute-start | bytes 1179656 | tf_op jit(solution)/shard_map/ppermute | solution.py:255
  5.1 16.6 %collective-permute-start.1 = (bf16[768,256]{1,0:T(8,128)(2,1)S(1)}, bf16[768,256]{1,0:T(8,128)(2,1)S(1)}, u32[]{:S(2)}, u32[]{:S(2)}) collective-permute-start(bf16[768,256]{1,0:T(8,128)(2,1)S(1)} %get-tuple-element.15), channel_id=1, source_target_pairs={{4,8},{8,4},{12,16},{16,12},{20,24},{24,20},{28,32},{32,28},{36,40... | collective-permute-start | bytes 1179656 | tf_op jit(solution)/shard_map/ppermute | solution.py:254
  11.4 1.4 %copy-start.8 = (bf16[48,64,192]{2,1,0:T(8,128)(2,1)S(1)}, bf16[48,64,192]{2,1,0:T(8,128)(2,1)}, u32[]{:S(2)}) copy-start(bf16[48,64,192]{2,1,0:T(8,128)(2,1)} %r_hbm.1) | copy-start | bytes 3538948
  21.7 26.2 %copy-start.7 = (s32[4,1]{0,1:T(1,128)S(1)}, s32[4,1]{0,1:T(1,128)}, u32[]{:S(2)}) copy-start(s32[4,1]{0,1:T(1,128)} %param.19) | copy-start | bytes 52
  36.4 2.5 %collective-permute-start.2 = (bf16[272,768]{1,0:T(8,128)(2,1)S(1)}, bf16[272,768]{1,0:T(8,128)(2,1)S(1)}, u32[]{:S(2)}, u32[]{:S(2)}) collective-permute-start(bf16[272,768]{1,0:T(8,128)(2,1)S(1)} %get-tuple-element.18), channel_id=1, source_target_pairs={{0,4},{4,0},{8,12},{12,8},{16,20},{20,16},{24,28},{28,24},{32,36},... | collective-permute-start | bytes 1253384 | tf_op jit(solution)/shard_map/ppermute | solution.py:255
  36.5 11.5 %collective-permute-start.3 = (bf16[272,768]{1,0:T(8,128)(2,1)S(1)}, bf16[272,768]{1,0:T(8,128)(2,1)S(1)}, u32[]{:S(2)}, u32[]{:S(2)}) collective-permute-start(bf16[272,768]{1,0:T(8,128)(2,1)S(1)} %get-tuple-element.19), channel_id=1, source_target_pairs={{4,8},{8,4},{12,16},{16,12},{20,24},{24,20},{28,32},{32,28},{36,40... | collective-permute-start | bytes 1253384 | tf_op jit(solution)/shard_map/ppermute | solution.py:254
  48.9 11.8 %collective-permute-start.4 = (bf16[144,1280]{1,0:T(8,128)(2,1)S(1)}, bf16[144,1280]{1,0:T(8,128)(2,1)S(1)}, u32[]{:S(2)}, u32[]{:S(2)}) collective-permute-start(bf16[144,1280]{1,0:T(8,128)(2,1)S(1)} %get-tuple-element.23), channel_id=1, source_target_pairs={{0,1},{1,2},{2,3},{3,0},{4,5},{5,6},{6,7},{7,4},{8,9},{9,10},{10,1... | collective-permute-start | bytes 1105928 | tf_op jit(solution)/shard_map/ppermute | solution.py:319
  50.4 17.8 %collective-permute-start.5 = (bf16[144,1280]{1,0:T(8,128)(2,1)S(1)}, bf16[144,1280]{1,0:T(8,128)(2,1)S(1)}, u32[]{:S(2)}, u32[]{:S(2)}) collective-permute-start(bf16[144,1280]{1,0:T(8,128)(2,1)S(1)} %get-tuple-element.24), channel_id=1, source_target_pairs={{0,2},{1,3},{2,0},{3,1},{4,6},{5,7},{6,4},{7,5},{8,10},{9,11},{10,... | collective-permute-start | bytes 1105928 | tf_op jit(solution)/shard_map/ppermute | solution.py:319
  53.1 15.0 %collective-permute-start.6 = (bf16[144,1280]{1,0:T(8,128)(2,1)S(1)}, bf16[144,1280]{1,0:T(8,128)(2,1)S(1)}, u32[]{:S(2)}, u32[]{:S(2)}) collective-permute-start(bf16[144,1280]{1,0:T(8,128)(2,1)S(1)} %get-tuple-element.25), channel_id=1, source_target_pairs={{0,3},{1,0},{2,1},{3,2},{4,7},{5,4},{6,5},{7,6},{8,11},{9,8},{10,9... | collective-permute-start | bytes 1105928 | tf_op jit(solution)/shard_map/ppermute | solution.py:319

commit v2 on v1

--- a/solution.py
+++ b/solution.py
@@ -10,9 +10,13 @@
 BF = jnp.bfloat16
 F32 = jnp.float32
 MIB = 1 << 20
-
-
-def params(mib=48):
+K1_MIB = 54
+K1_FLOPS = 20 * 10**9
+K2_MIB = 24
+HS = [slice(0, 768)]
+
+
+def params(mib=24):
     return pltpu.CompilerParams(vmem_limit_bytes=mib * MIB)
 
 
@@ -42,34 +46,34 @@
     return tiles
 
 
-def send_kernel(pcol, up, down, par, p_ref, out_a, out_b, *, coarse):
-    width = p_ref.shape[1]
+def send_kernel(pcol_hbm, up_hbm, down_hbm, par, p_hbm, out_a, out_b, pcol, up, down, p_v, sems, *, coarse):
+    width = p_v.shape[1]
+    copies = [
+        pltpu.make_async_copy(source, target, sems.at[n])
+        for n, (source, target) in enumerate(
+            ((pcol_hbm, pcol), (up_hbm, up), (down_hbm, down), (p_hbm, p_v)))
+    ]
+    for copy in copies:
+        copy.start()
     half = half_of_lane()
     even = par[0] == 0
+    for copy in copies:
+        copy.wait()
     for i in range(up.shape[0]):
         for out, first, second in ((out_b, down, up), (out_a, up, down)):
             f = jnp.where(even, first[i], second[i])
             cols = [pcol[q, f] for q in range(pcol.shape[0])]
-            tiles = dense_row(p_ref[f], cols, half, coarse)
+            tiles = dense_row(p_v[f], cols, half, coarse)
             for t, tile in enumerate(tiles):
                 out[i * width : (i + 1) * width, t * 128 : (t + 1) * 128] = tile
 
 
-def own_kernel(
-    acol, pcol, rcol, a_hbm, p_hbm, r_hbm, v_ref, ap_out, rd_out, a_v, p_v, r_v, table, sems, *, coarse
-):
+def own_kernel(acol, pcol, rcol, a_v, p_v, r_v, v_ref, ap_out, rd_out, spread_out, named, table, *, coarse):
     rows, width = a_v.shape[0], a_v.shape[1]
     kas, krs = acol.shape[0], rcol.shape[0]
-    copies = [
-        pltpu.make_async_copy(p_hbm, p_v, sems.at[0]),
-        pltpu.make_async_copy(r_hbm, r_v, sems.at[1]),
-        pltpu.make_async_copy(a_hbm, a_v, sems.at[2]),
-    ]
-    for copy in copies:
-        copy.start()
+    ghosts = rows // 4
     half = half_of_lane()
     table[rows * width :, :] = jnp.zeros((width, coarse * width), BF)
-    copies[0].wait()
 
     def densify(f, _):
         cols = [pcol[q, f] for q in range(pcol.shape[0])]
@@ -79,7 +83,26 @@
         return 0
 
     lax.fori_loop(0, rows, densify, 0, unroll=4)
-    copies[1].wait()
+
+    def apply(f, count):
+        picked = []
+        sides = [jnp.int32(0), jnp.int32(0)]
+        for k in range(kas):
+            c = acol[k, f]
+            if k > 0:
+                sides[0] = jnp.where((c >= rows) & (c < rows + ghosts), 1, sides[0])
+                sides[1] = jnp.where(c >= rows + ghosts, 1, sides[1])
+            c = jnp.where(c < rows, c, rows)
+            picked.append(table[pl.ds(pl.multiple_of(c * width, width), width), :])
+        strip = jnp.dot(a_v[f], jnp.concatenate(picked, 0), preferred_element_type=F32)
+        ap_out[pl.ds(pl.multiple_of(f * width, width), width), :] = strip.astype(BF)
+        for side in (0, 1):
+            named[count] = f + 64 * side
+            count = count + sides[side]
+        return count
+
+    named[127] = lax.fori_loop(0, rows, apply, jnp.int32(0), unroll=8)
+
     right = lax.broadcasted_iota(jnp.int32, (width, 128), 1) >= width
     for pair in range(rows // 2):
         lanes = slice(pair * 128, (pair + 1) * 128)
@@ -95,85 +118,81 @@
                 term = jnp.where(name == jnp.asarray(s, BF), block, jnp.zeros_like(block))
                 total = term if total is None else total + term
             rd_out[s * width : (s + 1) * width, lanes] = total
-    copies[2].wait()
-
-    def apply(f, _):
-        picked = []
-        for k in range(kas):
-            c = acol[k, f]
-            c = jnp.where(c < rows, c, rows)
-            picked.append(table[pl.ds(pl.multiple_of(c * width, width), width), :])
-        strip = jnp.dot(a_v[f], jnp.concatenate(picked, 0), preferred_element_type=F32)
-        ap_out[pl.ds(pl.multiple_of(f * width, width), width), :] = strip.astype(BF)
-        return 0
-
-    lax.fori_loop(0, rows, apply, 0, unroll=8)
+
+    flat = jnp.concatenate([v_ref[...].astype(F32), jnp.zeros((128 - rows, 2 * width), F32)], 0)
+    turned = flat.T
+    lane = lax.broadcasted_iota(jnp.int32, (width, 128), 1)
+    both = jnp.where(lane < width, turned[:width], pltpu.roll(turned[width:], width, 1))
+    at_lane = lane % width
+    for f in range(rows):
+        spread_out[f * width : (f + 1) * width, :] = jnp.where(at_lane == f, both, 0.0).astype(BF)
+
+
+def spread_sums(spread, seg, width):
+    pieces = []
+    for n in range(seg // 128):
+        t = spread[n * 128 : (n + 1) * 128].T
+        pieces.append(jnp.concatenate(
+            [jnp.sum(t[i * width : (i + 1) * width], 0, keepdims=True) for i in range(2)], 0))
+    vec = jnp.concatenate(pieces, 1)
+    return jnp.concatenate([vec, jnp.zeros((14, seg), F32)], 0)
 
 
 def ghost_kernel(
-    acol, par, got_a, got_b, a_hbm, rd_ref, ap_ref, v_ref, send_a, send_b, own, own_vec,
-    a_v, table, strips, sems, *, coarse
+    acol, named, par, got_a, got_b, a_v, rd_ref, ap_ref, spread_ref, send_a, send_b, own, own_vec,
+    strips, pieces, table, *, coarse
 ):
     rows, width = a_v.shape[0], a_v.shape[1]
     kas = acol.shape[0]
     ghosts = got_a.shape[0] // width
     seg = coarse * width
     block = ghosts * width
-    copy = pltpu.make_async_copy(a_hbm, a_v, sems.at[0])
-    copy.start()
     odd = par[0]
     table[pl.ds(pl.multiple_of((1 - odd) * block, block), block), :] = got_a[...]
     table[pl.ds(pl.multiple_of(odd * block, block), block), :] = got_b[...]
     table[2 * block :, :] = jnp.zeros((width, seg), BF)
-    strips[:, seg : 2 * seg] = ap_ref[...]
-
-    flat = jnp.concatenate([v_ref[...].astype(F32), jnp.zeros((128 - rows, 2 * width), F32)], 0)
-    turned = flat.T
-    lane = lax.broadcasted_iota(jnp.int32, (width, 128), 1)
-    both = jnp.where(lane < width, turned[:width], pltpu.roll(turned[width:], width, 1))
-    at_lane = lane % width
-    for f in range(rows):
-        strips[f * width : (f + 1) * width, 3 * seg :] = jnp.where(at_lane == f, both, 0.0).astype(BF)
-    copy.wait()
-
-    def apply(f, _):
-        at = pl.ds(pl.multiple_of(f * width, width), width)
-        cols = [acol[k, f] - rows for k in range(kas)]
-        for side in (0, 1):
+    strips[...] = jnp.zeros_like(strips)
+    count = named[127]
+    batch = 6
+
+    def apply(n, _):
+        for i in range(batch):
+            at = n * batch + i
+            code = named[jnp.minimum(at, 126)]
+            valid = at < count
+            side = jnp.where(valid, code // 64, 0)
+            f = jnp.where(valid, code % 64, 0)
             picked = []
             for k in range(kas):
-                c = cols[k]
-                inside = (c >= side * ghosts) & (c < (side + 1) * ghosts)
-                c = jnp.where(inside, c, 2 * ghosts)
+                c = acol[k, f] - rows - side * ghosts
+                c = jnp.where((c >= 0) & (c < ghosts), c + side * ghosts, 2 * ghosts)
                 picked.append(table[pl.ds(pl.multiple_of(c * width, width), width), :])
             strip = jnp.dot(a_v[f], jnp.concatenate(picked, 0), preferred_element_type=F32)
-            strips[at, side * 2 * seg : (side * 2 + 1) * seg] = strip.astype(BF)
+            into = jnp.where(valid, f, rows)
+            strips[side, pl.ds(pl.multiple_of(into * width, width), width), :] = strip.astype(BF)
         return 0
 
-    lax.fori_loop(0, rows, apply, 0, unroll=4)
-
-    def restrict(start, out, out_vec, kind):
-        r = rd_ref[pl.ds(pl.multiple_of(start, seg), seg), :]
-        for e in range(3):
-            lanes = slice(e * seg, (e + 1) * seg)
-            out[0:seg, lanes] = jnp.dot(r, strips[:, lanes], preferred_element_type=F32).astype(kind)
-        spread = jnp.dot(r, strips[:, 3 * seg :], preferred_element_type=F32)
-        pieces = []
-        for n in range(seg // 128):
-            t = spread[n * 128 : (n + 1) * 128].T
-            pieces.append(jnp.concatenate(
-                [jnp.sum(t[i * width : (i + 1) * width], 0, keepdims=True) for i in range(2)], 0))
-        vec = jnp.concatenate(pieces, 1)
-        vec = jnp.concatenate([vec, jnp.zeros((14, seg), F32)], 0).astype(kind)
-        if out_vec is None:
-            out[seg : seg + 16, 0:seg] = vec
-            out[seg : seg + 16, seg:] = jnp.zeros((16, 2 * seg), kind)
-        else:
-            out_vec[...] = vec
-
-    restrict(seg * 2 * (1 - odd), send_a, None, BF)
-    restrict(seg * 2 * odd, send_b, None, BF)
-    restrict(seg, own, own_vec, F32)
+    lax.fori_loop(0, (count + batch - 1) // batch, apply, 0)
+    deep = rows * width
+    parts = (strips[0, 0:deep], ap_ref[...], strips[1, 0:deep])
+    for e, part in enumerate(parts):
+        lanes = slice(e * seg, (e + 1) * seg)
+        for h in HS:
+            sums = jnp.dot(rd_ref[h], part, preferred_element_type=F32)
+            for n in range(sums.shape[0] // seg):
+                at = h.start // seg + n
+                block_sums = sums[n * seg : (n + 1) * seg]
+                if at == 1:
+                    own[:, lanes] = block_sums
+                else:
+                    pieces[at // 2, 0:seg, lanes] = block_sums.astype(BF)
+    sums = jnp.dot(rd_ref[...], spread_ref[...], preferred_element_type=F32)
+    own_vec[...] = spread_sums(sums[seg : 2 * seg], seg, width)
+    for n in range(2):
+        pieces[n, seg:, 0:seg] = spread_sums(sums[2 * n * seg : (2 * n + 1) * seg], seg, width).astype(BF)
+        pieces[n, seg:, seg:] = jnp.zeros((16, 2 * seg), BF)
+    send_a[...] = pieces[1 - odd]
+    send_b[...] = pieces[odd]
 
 
 def sum_kernel(dest, par, comp, got_a, got_b, own, own_vec, *outs, coarse):
@@ -268,42 +287,48 @@
     out_a, out_b = pl.pallas_call(
         functools.partial(send_kernel, coarse=coarse),
         out_shape=[shape((ghosts * width, seg), BF)] * 2,
-        in_specs=[SM, SM, SM, SM, VM],
+        in_specs=[ANY, ANY, ANY, SM, ANY],
         out_specs=[VM, VM],
-        compiler_params=params(),
+        scratch_shapes=[
+            pltpu.SMEM(pcol.shape, jnp.int32),
+            pltpu.SMEM(sent_up.shape, jnp.int32),
+            pltpu.SMEM(sent_down.shape, jnp.int32),
+            pltpu.VMEM(p_blocks.shape, BF),
+            pltpu.SemaphoreType.DMA((4,)),
+        ],
+        compiler_params=params(K1_MIB),
+        cost_estimate=pl.CostEstimate(flops=K1_FLOPS, bytes_accessed=10**6, transcendentals=0),
         name="send_rows",
     )(pcol, sent_up, sent_down, par, p_blocks)
     got_a, got_b = exchange(out_a, out_b)
-    strips, r_dense = pl.pallas_call(
+    strips, r_dense, spread, named = pl.pallas_call(
         functools.partial(own_kernel, coarse=coarse),
-        out_shape=[shape((rows * width, seg), BF), shape((3 * seg, rows * width), BF)],
-        in_specs=[SM, SM, SM, ANY, ANY, ANY, VM],
-        out_specs=[VM, VM],
-        scratch_shapes=[
-            pltpu.VMEM(a_blocks.shape, BF),
-            pltpu.VMEM(p_blocks.shape, BF),
-            pltpu.VMEM(r_blocks.shape, BF),
-            pltpu.VMEM(((rows + 1) * width, seg), BF),
-            pltpu.SemaphoreType.DMA((3,)),
+        out_shape=[
+            shape((rows * width, seg), BF),
+            shape((3 * seg, rows * width), BF),
+            shape((rows * width, 128), BF),
+            shape((128,), jnp.int32),
         ],
-        compiler_params=params(),
+        in_specs=[SM, SM, SM, VM, VM, VM, VM],
+        out_specs=[VM, VM, VM, SM],
+        scratch_shapes=[pltpu.VMEM(((rows + 1) * width, seg), BF)],
+        compiler_params=params(K2_MIB),
         cost_estimate=pl.CostEstimate(flops=4 * 10**9, bytes_accessed=20 * 10**6, transcendentals=0),
         name="own_columns",
     )(acol, pcol, rcol, a_blocks, p_blocks, r_blocks, vectors)
     send_a, send_b, own, own_vec = pl.pallas_call(
         functools.partial(ghost_kernel, coarse=coarse),
         out_shape=[shape((seg + 16, 3 * seg), BF)] * 2 + [shape((seg, 3 * seg), F32), shape((16, seg), F32)],
-        in_specs=[SM, SM, VM, VM, ANY, VM, VM, VM],
+        in_specs=[SM, SM, SM, VM, VM, VM, VM, VM, VM],
         out_specs=[VM] * 4,
         scratch_shapes=[
-            pltpu.VMEM(a_blocks.shape, BF),
+            pltpu.VMEM((2, (rows + 1) * width, seg), BF),
+            pltpu.VMEM((2, seg + 16, 3 * seg), BF),
             pltpu.VMEM(((2 * ghosts + 1) * width, seg), BF),
-            pltpu.VMEM((rows * width, 3 * seg + 128), BF),
-            pltpu.SemaphoreType.DMA((1,)),
         ],
-        compiler_params=params(),
+        compiler_params=params(K2_MIB),
         name="ghost_columns",
-    )(acol, par, got_a, got_b, a_blocks, r_dense, strips, vectors)
+    )(acol, named, par, got_a, got_b, a_blocks, r_dense, strips, spread)
     from_a, from_b = exchange(send_a, send_b)
     outs = pl.pallas_call(
         functools.partial(sum_kernel, coarse=coarse),

time: 69.6 us -> 59.9 us (0.86)
  local copies, waits for them, and re-layouts: 4.82 us -> 0.04 us
  Pallas kernels: 26.5 us -> 22.1 us
    pallas_call x1, Pallas kernels: 14.6 us -> 9.68 us  [on_device(): pl.pallas_call(functools.partial(ghost_kernel, coarse=coarse), out_shape=...]
    unnamed x20 -> x16, local copies, waits for them, and re-layouts: 4.82 us -> 0.04 us
    pallas_call x1, Pallas kernels: 0.93 us -> 2.82 us  [on_device(): pl.pallas_call(functools.partial(send_kernel, coarse=coarse), out_shape=[...]
    pallas_call x1, Pallas kernels: 8.9 us -> 7.52 us  [on_device(): pl.pallas_call(functools.partial(own_kernel, coarse=coarse), out_shape=[s...]
  transfers between devices with their start and end apart: 7 -> 7, of which waited for: 3 -> 4; matrix products, arithmetic and copies ran while one was open for 0% -> 0% of each run, Pallas kernels for 13% -> 13%
where the time goes in v2:
time: 59.9 us; the launch traced here: 59.8 us
  Pallas kernels  22.1 us (37%)
  waiting for transfers between devices  22.1 us (37%)
  starting transfers between devices  14.7 us (25%)
  between operations  0.86 us (1%)
    ppermute x3, waiting for transfers between devices, on_device(): lax.ppermute(outs[distance], 'comp', [(i, (i + distance) % 4) for i in ra...  13.6 us
    pallas_call x1, Pallas kernels, on_device(): pl.pallas_call(functools.partial(ghost_kernel, coarse=coarse), out_shape=...  9.68 us
    ppermute x2, starting transfers between devices, exchange(): got_b = lax.ppermute(block_b, 'mesh', across)  9.18 us
    ppermute x2, waiting for transfers between devices, exchange(): got_b = lax.ppermute(block_b, 'mesh', across)  8.49 us
    pallas_call x1, Pallas kernels, on_device(): pl.pallas_call(functools.partial(own_kernel, coarse=coarse), out_shape=[s...  7.52 us
    ppermute x3, starting transfers between devices, on_device(): lax.ppermute(outs[distance], 'comp', [(i, (i + distance) % 4) for i in ra...  5.33 us
    pallas_call x1, Pallas kernels, on_device(): pl.pallas_call(functools.partial(send_kernel, coarse=coarse), out_shape=[...  2.82 us
  transfers between devices with their start and end apart: 7, of which 4 were waited for; matrix products, arithmetic and copies ran while one was open for 0% of the time, Pallas kernels for 13%

profile of v2, /device:TPU:24, one launch (start us, length us, event | category | flops | bytes accessed | tf_op | source)
XLA Modules:
  0.0 59.8 jit_solution(17303967341225357065)
XLA Ops:
  0.6 0.0 copy-start
  0.7 0.0 copy-start.1
  0.7 0.0 copy-start.3
  0.7 0.0 copy-start.4
  0.7 2.8 %send_rows.1 = (bf16[768,256]{1,0:T(8,128)(2,1)}, bf16[768,256]{1,0:T(8,128)(2,1)}) custom-call(s32[3,48]{1,0:T(4,128)} %bitcast.9, s32[12]{0:T(128)} %up_hbm.1, s32[12]{0:T(128)} %down_hbm.1, s32[1]{0:T(128)} %bitcast.2.par, bf16[48,64,192]{2,1,0:T(8,128)(2,1)} %p_hbm.1), custom_call_target="tpu_custom_call" | custom-call | flops 20000000000 | bytes 1000000 | tf_op jit(solution)/shard_map/send_rows/pallas_call | solution.py:287
  3.5 0.1 collective-permute-start
  3.6 6.2 %collective-permute-start.1 = (bf16[768,256]{1,0:T(8,128)(2,1)}, bf16[768,256]{1,0:T(8,128)(2,1)S(1)}, u32[]{:S(2)}, u32[]{:S(2)}) collective-permute-start(bf16[768,256]{1,0:T(8,128)(2,1)} %get-tuple-element.18), channel_id=1, source_target_pairs={{4,8},{8,4},{12,16},{16,12},{20,24},{24,20},{28,32},{32,28},{36,40... | collective-permute-start | bytes 1179656 | tf_op jit(solution)/shard_map/ppermute | solution.py:273
  9.9 7.5 %own_columns.1 = (bf16[3072,256]{1,0:T(8,128)(2,1)S(1)}, bf16[768,3072]{1,0:T(8,128)(2,1)S(1)}, bf16[3072,128]{1,0:T(8,128)(2,1)S(1)}, s32[128]{0:T(128)S(1)}) custom-call(s32[7,48]{1,0:T(8,128)S(1)} %bitcast.6, s32[3,48]{1,0:T(4,128)S(1)} %bitcast.10, s32[3,48]{1,0:T(4,128)S(1)} %bitcast.11, bf16[48,64,448]{2,1,0:T(8,128)(2,1)S(1)} %copy-done, ...), custom_call_target="tpu_custom_call" | custom-call | flops 4000000000 | bytes 20000000 | tf_op jit(solution)/shard_map/own_columns/pallas_call | solution.py:304
  17.5 0.0 collective-permute-done.got_a
  17.5 0.0 collective-permute-done.1.got_b
  17.5 0.0 copy-start.2
  17.5 9.7 %ghost_columns.1 = (bf16[272,768]{1,0:T(8,128)(2,1)S(1)}, bf16[272,768]{1,0:T(8,128)(2,1)S(1)}, f32[256,768]{1,0:T(8,128)S(1)}, f32[16,256]{1,0:T(8,128)S(1)}) custom-call(s32[7,48]{1,0:T(8,128)S(1)} %bitcast.7, s32[128]{0:T(128)S(1)} %get-tuple-element.16.named, s32[1]{0:T(128)} %bitcast.2.par, bf16[768,256]{1,0:T(8,128)(2,1)S(1)} %collective-permute-done.got_a, ...), custom_call_target="tpu_custom_call" | custom-call | tf_op jit(solution)/shard_map/ghost_columns/pallas_call | solution.py:319
  27.2 0.1 collective-permute-start.2
  27.3 3.0 %collective-permute-start.3 = (bf16[272,768]{1,0:T(8,128)(2,1)S(1)}, bf16[272,768]{1,0:T(8,128)(2,1)S(1)}, u32[]{:S(2)}, u32[]{:S(2)}) collective-permute-start(bf16[272,768]{1,0:T(8,128)(2,1)S(1)} %get-tuple-element.23), channel_id=1, source_target_pairs={{4,8},{8,4},{12,16},{16,12},{20,24},{24,20},{28,32},{32,28},{36,40... | collective-permute-start | bytes 1253384 | tf_op jit(solution)/shard_map/ppermute | solution.py:273
  30.2 0.0 collective-permute-done.2.got_a
  30.3 8.5 %collective-permute-done.3.got_b = bf16[272,768]{1,0:T(8,128)(2,1)S(1)} collective-permute-done((bf16[272,768]{1,0:T(8,128)(2,1)S(1)}, bf16[272,768]{1,0:T(8,128)(2,1)S(1)}, u32[]{:S(2)}, u32[]{:S(2)}) %collective-permute-start.3) | collective-permute-done | bytes 417824 | tf_op jit(solution)/shard_map/ppermute | solution.py:273
  38.7 0.9 %sum_rows.1 = (bf16[144,1280]{1,0:T(8,128)(2,1)S(1)}, bf16[144,1280]{1,0:T(8,128)(2,1)S(1)}, bf16[144,1280]{1,0:T(8,128)(2,1)S(1)}, bf16[144,1280]{1,0:T(8,128)(2,1)S(1)}) custom-call(s32[1,4]{1,0:T(1,128)S(1)} %bitcast.8, s32[1]{0:T(128)} %bitcast.2.par, s32[1]{0:T(128)} %bitcast.comp, bf16[272,768]{1,0:T(8,128)(2,1)S(1)} %collective-permute-done.2.got_a, ...), custom_call_target="tpu_custom_call" | custom-call | tf_op jit(solution)/shard_map/sum_rows/pallas_call | solution.py:333
  39.6 1.2 %collective-permute-start.4 = (bf16[144,1280]{1,0:T(8,128)(2,1)S(1)}, bf16[144,1280]{1,0:T(8,128)(2,1)S(1)}, u32[]{:S(2)}, u32[]{:S(2)}) collective-permute-start(bf16[144,1280]{1,0:T(8,128)(2,1)S(1)} %get-tuple-element.27), channel_id=1, source_target_pairs={{0,1},{1,2},{2,3},{3,0},{4,5},{5,6},{6,7},{7,4},{8,9},{9,10},{10,1... | collective-permute-start | bytes 1105928 | tf_op jit(solution)/shard_map/ppermute | solution.py:344
  40.8 2.3 %collective-permute-start.5 = (bf16[144,1280]{1,0:T(8,128)(2,1)S(1)}, bf16[144,1280]{1,0:T(8,128)(2,1)S(1)}, u32[]{:S(2)}, u32[]{:S(2)}) collective-permute-start(bf16[144,1280]{1,0:T(8,128)(2,1)S(1)} %get-tuple-element.28), channel_id=1, source_target_pairs={{0,2},{1,3},{2,0},{3,1},{4,6},{5,7},{6,4},{7,5},{8,10},{9,11},{10,... | collective-permute-start | bytes 1105928 | tf_op jit(solution)/shard_map/ppermute | solution.py:344
  43.1 1.8 %collective-permute-start.6 = (bf16[144,1280]{1,0:T(8,128)(2,1)S(1)}, bf16[144,1280]{1,0:T(8,128)(2,1)S(1)}, u32[]{:S(2)}, u32[]{:S(2)}) collective-permute-start(bf16[144,1280]{1,0:T(8,128)(2,1)S(1)} %get-tuple-element.29), channel_id=1, source_target_pairs={{0,3},{1,0},{2,1},{3,2},{4,7},{5,4},{6,5},{7,6},{8,11},{9,8},{10,9... | collective-permute-start | bytes 1105928 | tf_op jit(solution)/shard_map/ppermute | solution.py:344
  45.0 7.3 %collective-permute-done.4.refs_1_ = bf16[144,1280]{1,0:T(8,128)(2,1)S(1)} collective-permute-done((bf16[144,1280]{1,0:T(8,128)(2,1)S(1)}, bf16[144,1280]{1,0:T(8,128)(2,1)S(1)}, u32[]{:S(2)}, u32[]{:S(2)}) %collective-permute-start.4) | collective-permute-done | bytes 368672 | tf_op jit(solution)/shard_map/ppermute | solution.py:344
  52.3 5.9 %collective-permute-done.5.refs_2_ = bf16[144,1280]{1,0:T(8,128)(2,1)S(1)} collective-permute-done((bf16[144,1280]{1,0:T(8,128)(2,1)S(1)}, bf16[144,1280]{1,0:T(8,128)(2,1)S(1)}, u32[]{:S(2)}, u32[]{:S(2)}) %collective-permute-start.5) | collective-permute-done | bytes 368672 | tf_op jit(solution)/shard_map/ppermute | solution.py:344
  58.2 0.4 collective-permute-done.6.refs_3_
  58.6 1.1 %into_slots.1 = (bf16[8,64,1280]{2,1,0:T(8,128)(2,1)}, bf16[8,128]{1,0:T(8,128)(2,1)}) custom-call(s32[1]{0:T(128)} %bitcast.comp, bf16[144,1280]{1,0:T(8,128)(2,1)S(1)} %get-tuple-element.26.refs_0_, bf16[144,1280]{1,0:T(8,128)(2,1)S(1)} %collective-permute-done.4.refs_1_, bf16[144,1280]{1,0:T(8,128)(2,1)S(1)} %collective-permute-done.5.refs_2_, ...), custom_call_target="tpu_custom_call" | custom-call | tf_op jit(solution)/shard_map/into_slots/pallas_call | solution.py:345
  (11 shorter events, 0.0 us)
Async XLA Ops:
  0.6 9.2 %copy-start = (bf16[48,64,448]{2,1,0:T(8,128)(2,1)S(1)}, bf16[48,64,448]{2,1,0:T(8,128)(2,1)}, u32[]{:S(2)}) copy-start(bf16[48,64,448]{2,1,0:T(8,128)(2,1)} %a_v.3) | copy-start | bytes 8257540
  0.7 9.2 %copy-start.1 = (s32[48,7]{0,1:T(8,128)S(1)}, s32[48,7]{0,1:T(8,128)}, u32[]{:S(2)}) copy-start(s32[48,7]{0,1:T(8,128)} %param.11) | copy-start | bytes 4036
  0.7 9.2 %copy-start.3 = (bf16[48,64,192]{2,1,0:T(8,128)(2,1)S(1)}, bf16[48,64,192]{2,1,0:T(8,128)(2,1)}, u32[]{:S(2)}) copy-start(bf16[48,64,192]{2,1,0:T(8,128)(2,1)} %p_hbm.1) | copy-start | bytes 3538948
  0.7 9.2 %copy-start.4 = (bf16[48,64,192]{2,1,0:T(8,128)(2,1)S(1)}, bf16[48,64,192]{2,1,0:T(8,128)(2,1)}, u32[]{:S(2)}) copy-start(bf16[48,64,192]{2,1,0:T(8,128)(2,1)} %r_v.1) | copy-start | bytes 3538948
  0.7 9.2 %copy-start.5 = (bf16[48,128]{1,0:T(8,128)(2,1)S(1)}, bf16[48,128]{1,0:T(8,128)(2,1)}, u32[]{:S(2)}) copy-start(bf16[48,128]{1,0:T(8,128)(2,1)} %v_ref.1) | copy-start | bytes 36868
  0.7 9.2 %copy-start.6 = (s32[48,3]{0,1:T(4,128)S(1)}, s32[48,3]{0,1:T(4,128)}, u32[]{:S(2)}) copy-start(s32[48,3]{0,1:T(4,128)} %param.13) | copy-start | bytes 1732
  0.7 9.2 %copy-start.7 = (s32[48,3]{0,1:T(4,128)S(1)}, s32[48,3]{0,1:T(4,128)}, u32[]{:S(2)}) copy-start(s32[48,3]{0,1:T(4,128)} %param.15) | copy-start | bytes 1732
  3.5 13.9 %collective-permute-start = (bf16[768,256]{1,0:T(8,128)(2,1)}, bf16[768,256]{1,0:T(8,128)(2,1)S(1)}, u32[]{:S(2)}, u32[]{:S(2)}) collective-permute-start(bf16[768,256]{1,0:T(8,128)(2,1)} %get-tuple-element.17), channel_id=1, source_target_pairs={{0,4},{4,0},{8,12},{12,8},{16,20},{20,16},{24,28},{28,24},{32,36},... | collective-permute-start | bytes 1179656 | tf_op jit(solution)/shard_map/ppermute | solution.py:274
  3.6 13.8 %collective-permute-start.1 = (bf16[768,256]{1,0:T(8,128)(2,1)}, bf16[768,256]{1,0:T(8,128)(2,1)S(1)}, u32[]{:S(2)}, u32[]{:S(2)}) collective-permute-start(bf16[768,256]{1,0:T(8,128)(2,1)} %get-tuple-element.18), channel_id=1, source_target_pairs={{4,8},{8,4},{12,16},{16,12},{20,24},{24,20},{28,32},{32,28},{36,40... | collective-permute-start | bytes 1179656 | tf_op jit(solution)/shard_map/ppermute | solution.py:273
  17.5 21.3 %copy-start.2 = (s32[4,1]{0,1:T(1,128)S(1)}, s32[4,1]{0,1:T(1,128)}, u32[]{:S(2)}) copy-start(s32[4,1]{0,1:T(1,128)} %param.19) | copy-start | bytes 52
  27.2 3.1 %collective-permute-start.2 = (bf16[272,768]{1,0:T(8,128)(2,1)S(1)}, bf16[272,768]{1,0:T(8,128)(2,1)S(1)}, u32[]{:S(2)}, u32[]{:S(2)}) collective-permute-start(bf16[272,768]{1,0:T(8,128)(2,1)S(1)} %get-tuple-element.22), channel_id=1, source_target_pairs={{0,4},{4,0},{8,12},{12,8},{16,20},{20,16},{24,28},{28,24},{32,36},... | collective-permute-start | bytes 1253384 | tf_op jit(solution)/shard_map/ppermute | solution.py:274
  27.3 11.5 %collective-permute-start.3 = (bf16[272,768]{1,0:T(8,128)(2,1)S(1)}, bf16[272,768]{1,0:T(8,128)(2,1)S(1)}, u32[]{:S(2)}, u32[]{:S(2)}) collective-permute-start(bf16[272,768]{1,0:T(8,128)(2,1)S(1)} %get-tuple-element.23), channel_id=1, source_target_pairs={{4,8},{8,4},{12,16},{16,12},{20,24},{24,20},{28,32},{32,28},{36,40... | collective-permute-start | bytes 1253384 | tf_op jit(solution)/shard_map/ppermute | solution.py:273
  39.6 12.6 %collective-permute-start.4 = (bf16[144,1280]{1,0:T(8,128)(2,1)S(1)}, bf16[144,1280]{1,0:T(8,128)(2,1)S(1)}, u32[]{:S(2)}, u32[]{:S(2)}) collective-permute-start(bf16[144,1280]{1,0:T(8,128)(2,1)S(1)} %get-tuple-element.27), channel_id=1, source_target_pairs={{0,1},{1,2},{2,3},{3,0},{4,5},{5,6},{6,7},{7,4},{8,9},{9,10},{10,1... | collective-permute-start | bytes 1105928 | tf_op jit(solution)/shard_map/ppermute | solution.py:344
  40.8 17.4 %collective-permute-start.5 = (bf16[144,1280]{1,0:T(8,128)(2,1)S(1)}, bf16[144,1280]{1,0:T(8,128)(2,1)S(1)}, u32[]{:S(2)}, u32[]{:S(2)}) collective-permute-start(bf16[144,1280]{1,0:T(8,128)(2,1)S(1)} %get-tuple-element.28), channel_id=1, source_target_pairs={{0,2},{1,3},{2,0},{3,1},{4,6},{5,7},{6,4},{7,5},{8,10},{9,11},{10,... | collective-permute-start | bytes 1105928 | tf_op jit(solution)/shard_map/ppermute | solution.py:344
  43.1 15.5 %collective-permute-start.6 = (bf16[144,1280]{1,0:T(8,128)(2,1)S(1)}, bf16[144,1280]{1,0:T(8,128)(2,1)S(1)}, u32[]{:S(2)}, u32[]{:S(2)}) collective-permute-start(bf16[144,1280]{1,0:T(8,128)(2,1)S(1)} %get-tuple-element.29), channel_id=1, source_target_pairs={{0,3},{1,0},{2,1},{3,2},{4,7},{5,4},{6,5},{7,6},{8,11},{9,8},{10,9... | collective-permute-start | bytes 1105928 | tf_op jit(solution)/shard_map/ppermute | solution.py:344

commit v3 on v2

--- a/solution.py
+++ b/solution.py
@@ -13,7 +13,9 @@
 K1_MIB = 54
 K1_FLOPS = 20 * 10**9
 K2_MIB = 24
-HS = [slice(0, 768)]
+STASH = 30
+K3_FLOPS = 3 * 10**9
+K4_FLOPS = 3 * 10**9
 
 
 def params(mib=24):
@@ -48,11 +50,8 @@
 
 def send_kernel(pcol_hbm, up_hbm, down_hbm, par, p_hbm, out_a, out_b, pcol, up, down, p_v, sems, *, coarse):
     width = p_v.shape[1]
-    copies = [
-        pltpu.make_async_copy(source, target, sems.at[n])
-        for n, (source, target) in enumerate(
-            ((pcol_hbm, pcol), (up_hbm, up), (down_hbm, down), (p_hbm, p_v)))
-    ]
+    pairs = [(pcol_hbm, pcol), (up_hbm, up), (down_hbm, down), (p_hbm, p_v)]
+    copies = [pltpu.make_async_copy(source, target, sems.at[n]) for n, (source, target) in enumerate(pairs)]
     for copy in copies:
         copy.start()
     half = half_of_lane()
@@ -68,7 +67,7 @@
                 out[i * width : (i + 1) * width, t * 128 : (t + 1) * 128] = tile
 
 
-def own_kernel(acol, pcol, rcol, a_v, p_v, r_v, v_ref, ap_out, rd_out, spread_out, named, table, *, coarse):
+def own_kernel(acol, pcol, rcol, a_v, p_v, r_v, v_ref, ap_out, sides_out, home_out, spread_out, named, table, *, coarse):
     rows, width = a_v.shape[0], a_v.shape[1]
     kas, krs = acol.shape[0], rcol.shape[0]
     ghosts = rows // 4
@@ -117,7 +116,13 @@
             for block, name in zip(blocks, names):
                 term = jnp.where(name == jnp.asarray(s, BF), block, jnp.zeros_like(block))
                 total = term if total is None else total + term
-            rd_out[s * width : (s + 1) * width, lanes] = total
+            h, row = s // coarse, s % coarse * width
+            if h == 1:
+                into = pair // 2 * coarse * width + row
+                home_out[into : into + width, pair % 2 * 128 : (pair % 2 + 1) * 128] = total
+            else:
+                row = row + h // 2 * coarse * width
+                sides_out[row : row + width, lanes] = total
 
     flat = jnp.concatenate([v_ref[...].astype(F32), jnp.zeros((128 - rows, 2 * width), F32)], 0)
     turned = flat.T
@@ -139,14 +144,20 @@
 
 
 def ghost_kernel(
-    acol, named, par, got_a, got_b, a_v, rd_ref, ap_ref, spread_ref, send_a, send_b, own, own_vec,
-    strips, pieces, table, *, coarse
+    acol, named, par, got_a, got_b, a_v, rd_ref, home_ref, ap_ref, spread_ref, send_a, send_b, stash, strips, table, sems, *, coarse
 ):
     rows, width = a_v.shape[0], a_v.shape[1]
     kas = acol.shape[0]
     ghosts = got_a.shape[0] // width
     seg = coarse * width
     block = ghosts * width
+    deep = rows * width
+    stored = [
+        pltpu.make_async_copy(home_ref, stash.at[2, 0:deep], sems.at[0]),
+        pltpu.make_async_copy(spread_ref, stash.at[3, 0:deep, 0:128], sems.at[1]),
+    ]
+    for copy in stored:
+        copy.start()
     odd = par[0]
     table[pl.ds(pl.multiple_of((1 - odd) * block, block), block), :] = got_a[...]
     table[pl.ds(pl.multiple_of(odd * block, block), block), :] = got_b[...]
@@ -173,26 +184,41 @@
         return 0
 
     lax.fori_loop(0, (count + batch - 1) // batch, apply, 0)
-    deep = rows * width
-    parts = (strips[0, 0:deep], ap_ref[...], strips[1, 0:deep])
-    for e, part in enumerate(parts):
-        lanes = slice(e * seg, (e + 1) * seg)
-        for h in HS:
-            sums = jnp.dot(rd_ref[h], part, preferred_element_type=F32)
-            for n in range(sums.shape[0] // seg):
-                at = h.start // seg + n
-                block_sums = sums[n * seg : (n + 1) * seg]
-                if at == 1:
-                    own[:, lanes] = block_sums
-                else:
-                    pieces[at // 2, 0:seg, lanes] = block_sums.astype(BF)
-    sums = jnp.dot(rd_ref[...], spread_ref[...], preferred_element_type=F32)
-    own_vec[...] = spread_sums(sums[seg : 2 * seg], seg, width)
-    for n in range(2):
-        pieces[n, seg:, 0:seg] = spread_sums(sums[2 * n * seg : (2 * n + 1) * seg], seg, width).astype(BF)
-        pieces[n, seg:, seg:] = jnp.zeros((16, 2 * seg), BF)
-    send_a[...] = pieces[1 - odd]
-    send_b[...] = pieces[odd]
+    keep = pltpu.make_async_copy(strips, stash.at[0:2], sems.at[2])
+    keep.start()
+    parts = (strips[0, 0:deep], ap_ref[...], strips[1, 0:deep], spread_ref[...])
+    for start, send in ((odd, send_b), (1 - odd, send_a)):
+        restrict(rd_ref[pl.ds(pl.multiple_of(start * seg, seg), seg), :], parts, send, None)
+    for copy in stored + [keep]:
+        copy.wait()
+
+
+def home_kernel(stash, ap_ref, own, own_vec, rd_ref, spread_ref, strips, sems):
+    seg = own.shape[0]
+    deep = ap_ref.shape[0]
+    pairs = (
+        (stash.at[2, 0:deep], rd_ref), (stash.at[0:2], strips), (stash.at[3, 0:deep, 0:128], spread_ref))
+    copies = [pltpu.make_async_copy(source, target, sems.at[n]) for n, (source, target) in enumerate(pairs)]
+    for copy in copies:
+        copy.start()
+    for copy in copies:
+        copy.wait()
+    parts = (strips[0, 0:deep], ap_ref[...], strips[1, 0:deep], spread_ref[...])
+    r = jnp.concatenate([rd_ref[n * seg : (n + 1) * seg, :] for n in range(deep // seg)], 1)
+    restrict(r, parts, own, own_vec)
+
+
+def restrict(r, parts, out, out_vec):
+    seg = r.shape[0]
+    for e in range(3):
+        sums = jnp.dot(r, parts[e], preferred_element_type=F32)
+        out[0:seg, e * seg : (e + 1) * seg] = sums.astype(out.dtype)
+    vec = spread_sums(jnp.dot(r, parts[3], preferred_element_type=F32), seg, 64)
+    if out_vec is None:
+        out[seg : seg + 16, 0:seg] = vec.astype(out.dtype)
+        out[seg : seg + 16, seg:] = jnp.zeros((16, 2 * seg), out.dtype)
+    else:
+        out_vec[...] = vec
 
 
 def sum_kernel(dest, par, comp, got_a, got_b, own, own_vec, *outs, coarse):
@@ -220,15 +246,15 @@
         for s in range(coarse):
             hit = jnp.where(away[s] == distance, ranks[s], -1)
             block = block + jnp.where(row == hit, lines[s], 0.0)
-        out[2 * width :, 0:128] = block.astype(BF)
-        out[2 * width :, 128:] = jnp.zeros((16, 5 * seg - 128), BF)
+        out[0:16, 10 * seg :] = block.astype(BF)
+        out[16:, 10 * seg :] = jnp.zeros((width - 16, 128), BF)
         for k in range(2):
             source = jnp.int32(-1)
             for s in range(coarse):
                 source = jnp.where((away[s] == distance) & (ranks[s] == k), s, source)
-            into = slice(k * width, (k + 1) * width)
-
-            def fill(below, above, out=out, into=into, source=source):
+            first_lane = k * 5 * seg
+
+            def fill(below, above, out=out, first_lane=first_lane, source=source):
                 at = pl.ds(pl.multiple_of(jnp.maximum(source, 0) * width, width), width)
                 for u in range(5):
                     total = None
@@ -237,7 +263,7 @@
                         if 0 <= e < 3:
                             term = ref[at, e * seg : (e + 1) * seg].astype(F32)
                             total = term if total is None else total + term
-                    out[into, u * seg : (u + 1) * seg] = total.astype(BF)
+                    out[:, first_lane + u * seg : first_lane + (u + 1) * seg] = total.astype(BF)
 
             @pl.when((source >= 0) & odd)
             def _():
@@ -249,30 +275,31 @@
 
             @pl.when(source < 0)
             def _():
-                out[into, :] = jnp.zeros((width, 5 * seg), BF)
+                out[:, first_lane : first_lane + 5 * seg] = jnp.zeros((width, 5 * seg), BF)
 
 
 def gather_kernel(comp, *refs):
     parts, matrix, vectors = refs[:4], refs[4], refs[5]
-    width = matrix.shape[1]
+    wide = matrix.shape[2]
     row = lax.broadcasted_iota(jnp.int32, (8, 128), 0)
     total = jnp.zeros((8, 128), F32)
     for distance, part in enumerate(parts):
         source = lax.rem(comp[0] - distance + 4, 4)
+        lines = part[0:16, 2 * wide :].astype(F32)
         for k in range(2):
-            matrix[source * 2 + k] = part[k * width : (k + 1) * width, :]
-            line = part[2 * width :, 0:128].astype(F32)[k : k + 1]
-            total = total + jnp.where(row == source * 2 + k, line, 0.0)
+            matrix[source * 2 + k] = part[:, k * wide : (k + 1) * wide]
+            total = total + jnp.where(row == source * 2 + k, lines[k : k + 1], 0.0)
     vectors[...] = total.astype(BF)
 
 
-def exchange(block_a, block_b):
+def across(block):
     n = lax.axis_size("mesh")
-    within = [(i, i ^ 1) for i in range(n)]
-    across = [(i, i + 1 if i % 2 else i - 1) for i in range(1, n - 1)]
-    got_b = lax.ppermute(block_b, "mesh", across)
-    got_a = lax.ppermute(block_a, "mesh", within)
-    return got_a, got_b
+    return lax.ppermute(block, "mesh", [(i, i + 1 if i % 2 else i - 1) for i in range(1, n - 1)])
+
+
+def within(block):
+    n = lax.axis_size("mesh")
+    return lax.ppermute(block, "mesh", [(i, i ^ 1) for i in range(n)])
 
 
 def on_device(a_blocks, a_columns, p_blocks, p_columns, r_blocks, r_columns, sent_up, sent_down, vectors, coarse_dest):
@@ -300,39 +327,56 @@
         cost_estimate=pl.CostEstimate(flops=K1_FLOPS, bytes_accessed=10**6, transcendentals=0),
         name="send_rows",
     )(pcol, sent_up, sent_down, par, p_blocks)
-    got_a, got_b = exchange(out_a, out_b)
-    strips, r_dense, spread, named = pl.pallas_call(
+    got_b, got_a = across(out_b), within(out_a)
+    strips, sides_dense, home_dense, spread, named = pl.pallas_call(
         functools.partial(own_kernel, coarse=coarse),
         out_shape=[
             shape((rows * width, seg), BF),
-            shape((3 * seg, rows * width), BF),
+            shape((2 * seg, rows * width), BF),
+            shape((rows * width, seg), BF),
             shape((rows * width, 128), BF),
             shape((128,), jnp.int32),
         ],
         in_specs=[SM, SM, SM, VM, VM, VM, VM],
-        out_specs=[VM, VM, VM, SM],
+        out_specs=[VM, VM, VM, VM, SM],
         scratch_shapes=[pltpu.VMEM(((rows + 1) * width, seg), BF)],
         compiler_params=params(K2_MIB),
         cost_estimate=pl.CostEstimate(flops=4 * 10**9, bytes_accessed=20 * 10**6, transcendentals=0),
         name="own_columns",
     )(acol, pcol, rcol, a_blocks, p_blocks, r_blocks, vectors)
-    send_a, send_b, own, own_vec = pl.pallas_call(
+    send_a, send_b, stash = pl.pallas_call(
         functools.partial(ghost_kernel, coarse=coarse),
-        out_shape=[shape((seg + 16, 3 * seg), BF)] * 2 + [shape((seg, 3 * seg), F32), shape((16, seg), F32)],
-        in_specs=[SM, SM, SM, VM, VM, VM, VM, VM, VM],
-        out_specs=[VM] * 4,
+        out_shape=[shape((seg + 16, 3 * seg), BF)] * 2 + [shape((STASH, (rows + 1) * width, seg), BF)],
+        in_specs=[SM, SM, SM] + [VM] * 7,
+        out_specs=[VM, VM, ANY],
         scratch_shapes=[
             pltpu.VMEM((2, (rows + 1) * width, seg), BF),
-            pltpu.VMEM((2, seg + 16, 3 * seg), BF),
             pltpu.VMEM(((2 * ghosts + 1) * width, seg), BF),
+            pltpu.SemaphoreType.DMA((3,)),
         ],
         compiler_params=params(K2_MIB),
+        cost_estimate=pl.CostEstimate(flops=K3_FLOPS, bytes_accessed=10**6, transcendentals=0),
         name="ghost_columns",
-    )(acol, named, par, got_a, got_b, a_blocks, r_dense, strips, spread)
-    from_a, from_b = exchange(send_a, send_b)
+    )(acol, named, par, got_a, got_b, a_blocks, sides_dense, home_dense, strips, spread)
+    from_b, from_a = across(send_b), within(send_a)
+    own, own_vec = pl.pallas_call(
+        home_kernel,
+        out_shape=[shape((seg, 3 * seg), F32), shape((16, seg), F32)],
+        in_specs=[ANY, VM],
+        out_specs=[VM] * 2,
+        scratch_shapes=[
+            pltpu.VMEM((rows * width, seg), BF),
+            pltpu.VMEM((rows * width, 128), BF),
+            pltpu.VMEM((2, (rows + 1) * width, seg), BF),
+            pltpu.SemaphoreType.DMA((3,)),
+        ],
+        compiler_params=params(K2_MIB),
+        cost_estimate=pl.CostEstimate(flops=K4_FLOPS, bytes_accessed=10**6, transcendentals=0),
+        name="home_rows",
+    )(stash, strips)
     outs = pl.pallas_call(
         functools.partial(sum_kernel, coarse=coarse),
-        out_shape=[shape((2 * width + 16, 5 * seg), BF)] * 4,
+        out_shape=[shape((width, 10 * seg + 128), BF)] * 4,
         in_specs=[SM, SM, SM, VM, VM, VM, VM],
         out_specs=[VM] * 4,
         compiler_params=params(),

time: 59.9 us -> 57 us (0.952)
  waiting for transfers between devices: 22.1 us -> 15.1 us
  starting transfers between devices: 14.7 us -> 16.9 us
  Pallas kernels: 22.1 us -> 23.9 us
    ppermute x4, waiting for transfers between devices: 8.49 us -> 2.55 us  [the longest x2 2.55 us: across(): lax.ppermute(block, 'mesh', [(i, i + 1 if i % 2 else i - 1) for i in rang...]
    pallas_call x0 -> x1, Pallas kernels: none -> 4.48 us  [on_device(): pl.pallas_call(home_kernel, out_shape=[shape((seg, 3 * seg), F32), shape(...]
    pallas_call x1, Pallas kernels: 9.68 us -> 7.26 us  [on_device(): pl.pallas_call(functools.partial(ghost_kernel, coarse=coarse), out_shape=...]
    ppermute x4, starting transfers between devices: 9.35 us -> 10.8 us  [the longest x2 10.6 us: across(): lax.ppermute(block, 'mesh', [(i, i + 1 if i % 2 else i - 1) for i in rang...]
    ppermute x3, waiting for transfers between devices: 13.6 us -> 12.6 us  [on_device(): lax.ppermute(outs[distance], 'comp', [(i, (i + distance) % 4) for i in ra...]
    ppermute x3, starting transfers between devices: 5.33 us -> 6.13 us  [on_device(): lax.ppermute(outs[distance], 'comp', [(i, (i + distance) % 4) for i in ra...]
  transfers between devices with their start and end apart: 7 -> 7, of which waited for: 4 -> 3; matrix products, arithmetic and copies ran while one was open for 0% -> 0% of each run, Pallas kernels for 13% -> 21%
where the time goes in v3:
time: 57 us; the launch traced here: 56.8 us
  Pallas kernels  23.9 us (42%)
  starting transfers between devices  16.9 us (30%)
  waiting for transfers between devices  15.1 us (26%)
  between operations  0.86 us (2%)
    ppermute x3, waiting for transfers between devices, on_device(): lax.ppermute(outs[distance], 'comp', [(i, (i + distance) % 4) for i in ra...  12.6 us
    ppermute x2, starting transfers between devices, across(): lax.ppermute(block, 'mesh', [(i, i + 1 if i % 2 else i - 1) for i in rang...  10.6 us
    pallas_call x1, Pallas kernels, on_device(): pl.pallas_call(functools.partial(own_kernel, coarse=coarse), out_shape=[s...  7.29 us
    pallas_call x1, Pallas kernels, on_device(): pl.pallas_call(functools.partial(ghost_kernel, coarse=coarse), out_shape=...  7.26 us
    ppermute x3, starting transfers between devices, on_device(): lax.ppermute(outs[distance], 'comp', [(i, (i + distance) % 4) for i in ra...  6.13 us
    pallas_call x1, Pallas kernels, on_device(): pl.pallas_call(home_kernel, out_shape=[shape((seg, 3 * seg), F32), shape(...  4.48 us
    pallas_call x1, Pallas kernels, on_device(): pl.pallas_call(functools.partial(send_kernel, coarse=coarse), out_shape=[...  2.82 us
    ppermute x2, waiting for transfers between devices, across(): lax.ppermute(block, 'mesh', [(i, i + 1 if i % 2 else i - 1) for i in rang...  2.55 us
  transfers between devices with their start and end apart: 7, of which 3 were waited for; matrix products, arithmetic and copies ran while one was open for 0% of the time, Pallas kernels for 21%

profile of v3, /device:TPU:24, one launch (start us, length us, event | category | flops | bytes accessed | tf_op | source)
XLA Modules:
  0.0 56.8 jit_solution(17640859434309019053)
XLA Ops:
  0.6 0.0 copy-start.1
  0.7 0.0 copy-start.2
  0.7 2.8 %send_rows.1 = (bf16[768,256]{1,0:T(8,128)(2,1)}, bf16[768,256]{1,0:T(8,128)(2,1)}) custom-call(s32[3,48]{1,0:T(4,128)} %bitcast.9, s32[12]{0:T(128)} %up_hbm.1, s32[12]{0:T(128)} %down_hbm.1, s32[1]{0:T(128)} %bitcast.2.par, bf16[48,64,192]{2,1,0:T(8,128)(2,1)} %p_hbm.1), custom_call_target="tpu_custom_call" | custom-call | flops 20000000000 | bytes 1000000 | tf_op jit(solution)/shard_map/send_rows/pallas_call | solution.py:314
  3.5 0.1 collective-permute-start
  3.6 6.2 %collective-permute-start.1 = (bf16[768,256]{1,0:T(8,128)(2,1)}, bf16[768,256]{1,0:T(8,128)(2,1)S(1)}, u32[]{:S(2)}, u32[]{:S(2)}) collective-permute-start(bf16[768,256]{1,0:T(8,128)(2,1)} %get-tuple-element.20), channel_id=1, source_target_pairs={{4,8},{8,4},{12,16},{16,12},{20,24},{24,20},{28,32},{32,28},{36,40... | collective-permute-start | bytes 1179656 | tf_op jit(solution)/shard_map/ppermute | solution.py:297
  9.9 7.3 %own_columns.1 = (bf16[3072,256]{1,0:T(8,128)(2,1)S(1)}, bf16[512,3072]{1,0:T(8,128)(2,1)S(1)}, bf16[3072,256]{1,0:T(8,128)(2,1)S(1)}, bf16[3072,128]{1,0:T(8,128)(2,1)S(1)}, s32[128]{0:T(128)S(1)}) custom-call(s32[7,48]{1,0:T(8,128)S(1)} %bitcast.7, s32[3,48]{1,0:T(4,128)S(1)} %bitcast.10, s32[3,48]{1,0:T(4,128)S(1)} %bitcast.11, ...), custom_call_target="tpu_custom_call" | custom-call | flops 4000000000 | bytes 20000000 | tf_op jit(solution)/shard_map/own_columns/pallas_call | solution.py:331
  17.2 0.0 collective-permute-done.got_a
  17.2 0.0 collective-permute-done.1.got_b
  17.2 7.3 %ghost_columns.1 = (bf16[272,768]{1,0:T(8,128)(2,1)S(1)}, bf16[272,768]{1,0:T(8,128)(2,1)S(1)}, bf16[30,3136,256]{2,1,0:T(8,128)(2,1)}) custom-call(s32[7,48]{1,0:T(8,128)S(1)} %bitcast.8, s32[128]{0:T(128)S(1)} %get-tuple-element.18.named, s32[1]{0:T(128)} %bitcast.2.par, bf16[768,256]{1,0:T(8,128)(2,1)S(1)} %collective-permute-done.got_a, ...), custom_call_target="tpu_custom_call" | custom-call | flops 3000000000 | bytes 1000000 | tf_op jit(solution)/shard_map/ghost_columns/pallas_call | solution.py:347
  24.5 0.1 collective-permute-start.2
  24.6 4.4 %collective-permute-start.3 = (bf16[272,768]{1,0:T(8,128)(2,1)S(1)}, bf16[272,768]{1,0:T(8,128)(2,1)S(1)}, u32[]{:S(2)}, u32[]{:S(2)}) collective-permute-start(bf16[272,768]{1,0:T(8,128)(2,1)S(1)} %get-tuple-element.26), channel_id=1, source_target_pairs={{4,8},{8,4},{12,16},{16,12},{20,24},{24,20},{28,32},{32,28},{36,40... | collective-permute-start | bytes 1253384 | tf_op jit(solution)/shard_map/ppermute | solution.py:297
  29.0 0.0 copy-start
  29.0 4.5 %home_rows.1 = (f32[256,768]{1,0:T(8,128)S(1)}, f32[16,256]{1,0:T(8,128)S(1)}) custom-call(bf16[30,3136,256]{2,1,0:T(8,128)(2,1)} %get-tuple-element.27.stash, bf16[3072,256]{1,0:T(8,128)(2,1)S(1)} %get-tuple-element.23.ap_ref), custom_call_target="tpu_custom_call" | custom-call | flops 3000000000 | bytes 1000000 | tf_op jit(solution)/shard_map/home_rows/pallas_call | solution.py:362
  33.5 0.0 collective-permute-done.2.got_a
  33.5 2.5 %collective-permute-done.3.got_b = bf16[272,768]{1,0:T(8,128)(2,1)S(1)} collective-permute-done((bf16[272,768]{1,0:T(8,128)(2,1)S(1)}, bf16[272,768]{1,0:T(8,128)(2,1)S(1)}, u32[]{:S(2)}, u32[]{:S(2)}) %collective-permute-start.3) | collective-permute-done | bytes 417824 | tf_op jit(solution)/shard_map/ppermute | solution.py:297
  36.1 0.0 copy-done
  36.1 0.9 %sum_rows.1 = (bf16[64,2688]{1,0:T(8,128)(2,1)S(1)}, bf16[64,2688]{1,0:T(8,128)(2,1)S(1)}, bf16[64,2688]{1,0:T(8,128)(2,1)S(1)}, bf16[64,2688]{1,0:T(8,128)(2,1)S(1)}) custom-call(s32[1,4]{1,0:T(1,128)S(1)} %bitcast.6, s32[1]{0:T(128)} %bitcast.2.par, s32[1]{0:T(128)} %bitcast.comp, bf16[272,768]{1,0:T(8,128)(2,1)S(1)} %collective-permute-done.2.got_a, ...), custom_call_target="tpu_custom_call" | custom-call | tf_op jit(solution)/shard_map/sum_rows/pallas_call | solution.py:377
  37.0 1.6 %collective-permute-start.4 = (bf16[64,2688]{1,0:T(8,128)(2,1)S(1)}, bf16[64,2688]{1,0:T(8,128)(2,1)S(1)}, u32[]{:S(2)}, u32[]{:S(2)}) collective-permute-start(bf16[64,2688]{1,0:T(8,128)(2,1)S(1)} %get-tuple-element.31), channel_id=1, source_target_pairs={{0,1},{1,2},{2,3},{3,0},{4,5},{5,6},{6,7},{7,4},{8,9},{9,10},{10,1... | collective-permute-start | bytes 1032200 | tf_op jit(solution)/shard_map/ppermute | solution.py:388
  38.5 3.1 %collective-permute-start.5 = (bf16[64,2688]{1,0:T(8,128)(2,1)S(1)}, bf16[64,2688]{1,0:T(8,128)(2,1)S(1)}, u32[]{:S(2)}, u32[]{:S(2)}) collective-permute-start(bf16[64,2688]{1,0:T(8,128)(2,1)S(1)} %get-tuple-element.32), channel_id=1, source_target_pairs={{0,2},{1,3},{2,0},{3,1},{4,6},{5,7},{6,4},{7,5},{8,10},{9,11},{10,... | collective-permute-start | bytes 1032200 | tf_op jit(solution)/shard_map/ppermute | solution.py:388
  41.7 1.4 %collective-permute-start.6 = (bf16[64,2688]{1,0:T(8,128)(2,1)S(1)}, bf16[64,2688]{1,0:T(8,128)(2,1)S(1)}, u32[]{:S(2)}, u32[]{:S(2)}) collective-permute-start(bf16[64,2688]{1,0:T(8,128)(2,1)S(1)} %get-tuple-element.33), channel_id=1, source_target_pairs={{0,3},{1,0},{2,1},{3,2},{4,7},{5,4},{6,5},{7,6},{8,11},{9,8},{10,9... | collective-permute-start | bytes 1032200 | tf_op jit(solution)/shard_map/ppermute | solution.py:388
  43.1 5.2 %collective-permute-done.4.refs_1_ = bf16[64,2688]{1,0:T(8,128)(2,1)S(1)} collective-permute-done((bf16[64,2688]{1,0:T(8,128)(2,1)S(1)}, bf16[64,2688]{1,0:T(8,128)(2,1)S(1)}, u32[]{:S(2)}, u32[]{:S(2)}) %collective-permute-start.4) | collective-permute-done | bytes 344096 | tf_op jit(solution)/shard_map/ppermute | solution.py:388
  48.3 7.4 %collective-permute-done.5.refs_2_ = bf16[64,2688]{1,0:T(8,128)(2,1)S(1)} collective-permute-done((bf16[64,2688]{1,0:T(8,128)(2,1)S(1)}, bf16[64,2688]{1,0:T(8,128)(2,1)S(1)}, u32[]{:S(2)}, u32[]{:S(2)}) %collective-permute-start.5) | collective-permute-done | bytes 344096 | tf_op jit(solution)/shard_map/ppermute | solution.py:388
  55.7 0.0 collective-permute-done.6.refs_3_
  55.7 1.1 %into_slots.1 = (bf16[8,64,1280]{2,1,0:T(8,128)(2,1)}, bf16[8,128]{1,0:T(8,128)(2,1)}) custom-call(s32[1]{0:T(128)} %bitcast.comp, bf16[64,2688]{1,0:T(8,128)(2,1)S(1)} %get-tuple-element.30.refs_0_, bf16[64,2688]{1,0:T(8,128)(2,1)S(1)} %collective-permute-done.4.refs_1_, bf16[64,2688]{1,0:T(8,128)(2,1)S(1)} %collective-permute-done.5.refs_2_, ...), custom_call_target="tpu_custom_call" | custom-call | tf_op jit(solution)/shard_map/into_slots/pallas_call | solution.py:389
  (12 shorter events, 0.0 us)
Async XLA Ops:
  0.6 9.2 %copy-start.1 = (bf16[48,64,448]{2,1,0:T(8,128)(2,1)S(1)}, bf16[48,64,448]{2,1,0:T(8,128)(2,1)}, u32[]{:S(2)}) copy-start(bf16[48,64,448]{2,1,0:T(8,128)(2,1)} %a_v.3) | copy-start | bytes 8257540
  0.7 9.2 %copy-start.2 = (bf16[48,64,192]{2,1,0:T(8,128)(2,1)S(1)}, bf16[48,64,192]{2,1,0:T(8,128)(2,1)}, u32[]{:S(2)}) copy-start(bf16[48,64,192]{2,1,0:T(8,128)(2,1)} %p_hbm.1) | copy-start | bytes 3538948
  0.7 9.2 %copy-start.3 = (bf16[48,64,192]{2,1,0:T(8,128)(2,1)S(1)}, bf16[48,64,192]{2,1,0:T(8,128)(2,1)}, u32[]{:S(2)}) copy-start(bf16[48,64,192]{2,1,0:T(8,128)(2,1)} %r_v.1) | copy-start | bytes 3538948
  0.7 9.2 %copy-start.4 = (bf16[48,128]{1,0:T(8,128)(2,1)S(1)}, bf16[48,128]{1,0:T(8,128)(2,1)}, u32[]{:S(2)}) copy-start(bf16[48,128]{1,0:T(8,128)(2,1)} %v_ref.1) | copy-start | bytes 36868
  0.7 9.2 %copy-start.5 = (s32[48,7]{0,1:T(8,128)S(1)}, s32[48,7]{0,1:T(8,128)}, u32[]{:S(2)}) copy-start(s32[48,7]{0,1:T(8,128)} %param.11) | copy-start | bytes 4036
  0.7 9.2 %copy-start.6 = (s32[48,3]{0,1:T(4,128)S(1)}, s32[48,3]{0,1:T(4,128)}, u32[]{:S(2)}) copy-start(s32[48,3]{0,1:T(4,128)} %param.13) | copy-start | bytes 1732
  0.7 9.2 %copy-start.7 = (s32[48,3]{0,1:T(4,128)S(1)}, s32[48,3]{0,1:T(4,128)}, u32[]{:S(2)}) copy-start(s32[48,3]{0,1:T(4,128)} %param.15) | copy-start | bytes 1732
  3.5 13.7 %collective-permute-start = (bf16[768,256]{1,0:T(8,128)(2,1)}, bf16[768,256]{1,0:T(8,128)(2,1)S(1)}, u32[]{:S(2)}, u32[]{:S(2)}) collective-permute-start(bf16[768,256]{1,0:T(8,128)(2,1)} %get-tuple-element.19), channel_id=1, source_target_pairs={{0,4},{4,0},{8,12},{12,8},{16,20},{20,16},{24,28},{28,24},{32,36},... | collective-permute-start | bytes 1179656 | tf_op jit(solution)/shard_map/ppermute | solution.py:302
  3.6 13.6 %collective-permute-start.1 = (bf16[768,256]{1,0:T(8,128)(2,1)}, bf16[768,256]{1,0:T(8,128)(2,1)S(1)}, u32[]{:S(2)}, u32[]{:S(2)}) collective-permute-start(bf16[768,256]{1,0:T(8,128)(2,1)} %get-tuple-element.20), channel_id=1, source_target_pairs={{4,8},{8,4},{12,16},{16,12},{20,24},{24,20},{28,32},{32,28},{36,40... | collective-permute-start | bytes 1179656 | tf_op jit(solution)/shard_map/ppermute | solution.py:297
  24.5 9.0 %collective-permute-start.2 = (bf16[272,768]{1,0:T(8,128)(2,1)S(1)}, bf16[272,768]{1,0:T(8,128)(2,1)S(1)}, u32[]{:S(2)}, u32[]{:S(2)}) collective-permute-start(bf16[272,768]{1,0:T(8,128)(2,1)S(1)} %get-tuple-element.25), channel_id=1, source_target_pairs={{0,4},{4,0},{8,12},{12,8},{16,20},{20,16},{24,28},{28,24},{32,36},... | collective-permute-start | bytes 1253384 | tf_op jit(solution)/shard_map/ppermute | solution.py:302
  24.6 11.5 %collective-permute-start.3 = (bf16[272,768]{1,0:T(8,128)(2,1)S(1)}, bf16[272,768]{1,0:T(8,128)(2,1)S(1)}, u32[]{:S(2)}, u32[]{:S(2)}) collective-permute-start(bf16[272,768]{1,0:T(8,128)(2,1)S(1)} %get-tuple-element.26), channel_id=1, source_target_pairs={{4,8},{8,4},{12,16},{16,12},{20,24},{24,20},{28,32},{32,28},{36,40... | collective-permute-start | bytes 1253384 | tf_op jit(solution)/shard_map/ppermute | solution.py:297
  29.0 7.1 %copy-start = (s32[4,1]{0,1:T(1,128)S(1)}, s32[4,1]{0,1:T(1,128)}, u32[]{:S(2)}) copy-start(s32[4,1]{0,1:T(1,128)} %param.19) | copy-start | bytes 52
  37.0 11.3 %collective-permute-start.4 = (bf16[64,2688]{1,0:T(8,128)(2,1)S(1)}, bf16[64,2688]{1,0:T(8,128)(2,1)S(1)}, u32[]{:S(2)}, u32[]{:S(2)}) collective-permute-start(bf16[64,2688]{1,0:T(8,128)(2,1)S(1)} %get-tuple-element.31), channel_id=1, source_target_pairs={{0,1},{1,2},{2,3},{3,0},{4,5},{5,6},{6,7},{7,4},{8,9},{9,10},{10,1... | collective-permute-start | bytes 1032200 | tf_op jit(solution)/shard_map/ppermute | solution.py:388
  38.5 17.1 %collective-permute-start.5 = (bf16[64,2688]{1,0:T(8,128)(2,1)S(1)}, bf16[64,2688]{1,0:T(8,128)(2,1)S(1)}, u32[]{:S(2)}, u32[]{:S(2)}) collective-permute-start(bf16[64,2688]{1,0:T(8,128)(2,1)S(1)} %get-tuple-element.32), channel_id=1, source_target_pairs={{0,2},{1,3},{2,0},{3,1},{4,6},{5,7},{6,4},{7,5},{8,10},{9,11},{10,... | collective-permute-start | bytes 1032200 | tf_op jit(solution)/shard_map/ppermute | solution.py:388
  41.7 14.0 %collective-permute-start.6 = (bf16[64,2688]{1,0:T(8,128)(2,1)S(1)}, bf16[64,2688]{1,0:T(8,128)(2,1)S(1)}, u32[]{:S(2)}, u32[]{:S(2)}) collective-permute-start(bf16[64,2688]{1,0:T(8,128)(2,1)S(1)} %get-tuple-element.33), channel_id=1, source_target_pairs={{0,3},{1,0},{2,1},{3,2},{4,7},{5,4},{6,5},{7,6},{8,11},{9,8},{10,9... | collective-permute-start | bytes 1032200 | tf_op jit(solution)/shard_map/ppermute | solution.py:388

commit v4 on v3

--- a/solution.py
+++ b/solution.py
@@ -67,7 +67,7 @@
                 out[i * width : (i + 1) * width, t * 128 : (t + 1) * 128] = tile
 
 
-def own_kernel(acol, pcol, rcol, a_v, p_v, r_v, v_ref, ap_out, sides_out, home_out, spread_out, named, table, *, coarse):
+def own_kernel(acol, pcol, rcol, a_v, p_v, r_v, v_ref, ap_out, sides_out, home_out, spread_out, mid_out, vec_out, named, table, *, coarse):
     rows, width = a_v.shape[0], a_v.shape[1]
     kas, krs = acol.shape[0], rcol.shape[0]
     ghosts = rows // 4
@@ -81,7 +81,7 @@
             table[at, t * 128 : (t + 1) * 128] = tile
         return 0
 
-    lax.fori_loop(0, rows, densify, 0, unroll=4)
+    lax.fori_loop(0, rows, densify, 0, unroll=16)
 
     def apply(f, count):
         picked = []
@@ -100,7 +100,7 @@
             count = count + sides[side]
         return count
 
-    named[127] = lax.fori_loop(0, rows, apply, jnp.int32(0), unroll=8)
+    named[127] = lax.fori_loop(0, rows, apply, jnp.int32(0), unroll=48)
 
     right = lax.broadcasted_iota(jnp.int32, (width, 128), 1) >= width
     for pair in range(rows // 2):
@@ -132,6 +132,14 @@
     for f in range(rows):
         spread_out[f * width : (f + 1) * width, :] = jnp.where(at_lane == f, both, 0.0).astype(BF)
 
+    seg = coarse * width
+    for side in (0, 1):
+        at = slice(side * seg, (side + 1) * seg)
+        r = sides_out[at, :]
+        mid_out[at, :] = jnp.dot(r, ap_out[...], preferred_element_type=F32).astype(BF)
+        sums = jnp.dot(r, spread_out[...], preferred_element_type=F32)
+        vec_out[side * 16 : (side + 1) * 16, :] = spread_sums(sums, seg, width).astype(BF)
+
 
 def spread_sums(spread, seg, width):
     pieces = []
@@ -144,7 +152,7 @@
 
 
 def ghost_kernel(
-    acol, named, par, got_a, got_b, a_v, rd_ref, home_ref, ap_ref, spread_ref, send_a, send_b, stash, strips, table, sems, *, coarse
+    acol, named, par, got_a, got_b, a_v, rd_ref, home_ref, mid_ref, vec_ref, spread_ref, send_a, send_b, stash, strips, table, sems, *, coarse
 ):
     rows, width = a_v.shape[0], a_v.shape[1]
     kas = acol.shape[0]
@@ -164,7 +172,7 @@
     table[2 * block :, :] = jnp.zeros((width, seg), BF)
     strips[...] = jnp.zeros_like(strips)
     count = named[127]
-    batch = 6
+    batch = 20
 
     def apply(n, _):
         for i in range(batch):
@@ -186,9 +194,15 @@
     lax.fori_loop(0, (count + batch - 1) // batch, apply, 0)
     keep = pltpu.make_async_copy(strips, stash.at[0:2], sems.at[2])
     keep.start()
-    parts = (strips[0, 0:deep], ap_ref[...], strips[1, 0:deep], spread_ref[...])
     for start, send in ((odd, send_b), (1 - odd, send_a)):
-        restrict(rd_ref[pl.ds(pl.multiple_of(start * seg, seg), seg), :], parts, send, None)
+        at = pl.ds(pl.multiple_of(start * seg, seg), seg)
+        r = rd_ref[at, :]
+        for side in (0, 1):
+            sums = jnp.dot(r, strips[side, 0:deep], preferred_element_type=F32)
+            send[0:seg, 2 * side * seg : (2 * side + 1) * seg] = sums.astype(BF)
+        send[0:seg, seg : 2 * seg] = mid_ref[at, :]
+        send[seg:, 0:seg] = vec_ref[pl.ds(pl.multiple_of(start * 16, 16), 16), :]
+        send[seg:, seg:] = jnp.zeros((16, 2 * seg), BF)
     for copy in stored + [keep]:
         copy.wait()
 
@@ -214,11 +228,7 @@
         sums = jnp.dot(r, parts[e], preferred_element_type=F32)
         out[0:seg, e * seg : (e + 1) * seg] = sums.astype(out.dtype)
     vec = spread_sums(jnp.dot(r, parts[3], preferred_element_type=F32), seg, 64)
-    if out_vec is None:
-        out[seg : seg + 16, 0:seg] = vec.astype(out.dtype)
-        out[seg : seg + 16, seg:] = jnp.zeros((16, 2 * seg), out.dtype)
-    else:
-        out_vec[...] = vec
+    out_vec[...] = vec
 
 
 def sum_kernel(dest, par, comp, got_a, got_b, own, own_vec, *outs, coarse):
@@ -328,17 +338,19 @@
         name="send_rows",
     )(pcol, sent_up, sent_down, par, p_blocks)
     got_b, got_a = across(out_b), within(out_a)
-    strips, sides_dense, home_dense, spread, named = pl.pallas_call(
+    strips, sides_dense, home_dense, spread, mid, side_vec, named = pl.pallas_call(
         functools.partial(own_kernel, coarse=coarse),
         out_shape=[
             shape((rows * width, seg), BF),
             shape((2 * seg, rows * width), BF),
             shape((rows * width, seg), BF),
             shape((rows * width, 128), BF),
+            shape((2 * seg, seg), BF),
+            shape((32, seg), BF),
             shape((128,), jnp.int32),
         ],
         in_specs=[SM, SM, SM, VM, VM, VM, VM],
-        out_specs=[VM, VM, VM, VM, SM],
+        out_specs=[VM] * 6 + [SM],
         scratch_shapes=[pltpu.VMEM(((rows + 1) * width, seg), BF)],
         compiler_params=params(K2_MIB),
         cost_estimate=pl.CostEstimate(flops=4 * 10**9, bytes_accessed=20 * 10**6, transcendentals=0),
@@ -347,7 +359,7 @@
     send_a, send_b, stash = pl.pallas_call(
         functools.partial(ghost_kernel, coarse=coarse),
         out_shape=[shape((seg + 16, 3 * seg), BF)] * 2 + [shape((STASH, (rows + 1) * width, seg), BF)],
-        in_specs=[SM, SM, SM] + [VM] * 7,
+        in_specs=[SM, SM, SM] + [VM] * 8,
         out_specs=[VM, VM, ANY],
         scratch_shapes=[
             pltpu.VMEM((2, (rows + 1) * width, seg), BF),
@@ -357,7 +369,7 @@
         compiler_params=params(K2_MIB),
         cost_estimate=pl.CostEstimate(flops=K3_FLOPS, bytes_accessed=10**6, transcendentals=0),
         name="ghost_columns",
-    )(acol, named, par, got_a, got_b, a_blocks, sides_dense, home_dense, strips, spread)
+    )(acol, named, par, got_a, got_b, a_blocks, sides_dense, home_dense, mid, side_vec, spread)
     from_b, from_a = across(send_b), within(send_a)
     own, own_vec = pl.pallas_call(
         home_kernel,

time: 57 us -> 54.3 us (0.953)
  Pallas kernels: 23.9 us -> 21.7 us
  waiting for transfers between devices: 15.1 us -> 14.5 us
    pallas_call x1, Pallas kernels: 7.26 us -> 5.71 us  [on_device(): pl.pallas_call(functools.partial(ghost_kernel, coarse=coarse), out_shape=...]
    pallas_call x1, Pallas kernels: 7.29 us -> 6.62 us  [on_device(): pl.pallas_call(functools.partial(own_kernel, coarse=coarse), out_shape=[s...]
  transfers between devices with their start and end apart: 7 -> 7, of which waited for: 3 -> 4; matrix products, arithmetic and copies ran while one was open for 0% -> 0% of each run, Pallas kernels for 21% -> 21%
where the time goes in v4:
time: 54.3 us; the launch traced here: 53.8 us
  Pallas kernels  21.7 us (40%)
  starting transfers between devices  16.8 us (31%)
  waiting for transfers between devices  14.5 us (27%)
  between operations  0.86 us (2%)
    ppermute x3, waiting for transfers between devices, on_device(): lax.ppermute(outs[distance], 'comp', [(i, (i + distance) % 4) for i in ra...  12.2 us
    ppermute x2, starting transfers between devices, across(): lax.ppermute(block, 'mesh', [(i, i + 1 if i % 2 else i - 1) for i in rang...  10.9 us
    pallas_call x1, Pallas kernels, on_device(): pl.pallas_call(functools.partial(own_kernel, coarse=coarse), out_shape=[s...  6.62 us
    ppermute x3, starting transfers between devices, on_device(): lax.ppermute(outs[distance], 'comp', [(i, (i + distance) % 4) for i in ra...  5.73 us
    pallas_call x1, Pallas kernels, on_device(): pl.pallas_call(functools.partial(ghost_kernel, coarse=coarse), out_shape=...  5.71 us
    pallas_call x1, Pallas kernels, on_device(): pl.pallas_call(home_kernel, out_shape=[shape((seg, 3 * seg), F32), shape(...  4.48 us
    pallas_call x1, Pallas kernels, on_device(): pl.pallas_call(functools.partial(send_kernel, coarse=coarse), out_shape=[...  2.82 us
    ppermute x2, waiting for transfers between devices, across(): lax.ppermute(block, 'mesh', [(i, i + 1 if i % 2 else i - 1) for i in rang...  2.28 us
  transfers between devices with their start and end apart: 7, of which 4 were waited for; matrix products, arithmetic and copies ran while one was open for 0% of the time, Pallas kernels for 21%

profile of v4, /device:TPU:24, one launch (start us, length us, event | category | flops | bytes accessed | tf_op | source)
XLA Modules:
  0.0 53.8 jit_solution(1979389289120663042)
XLA Ops:
  0.6 0.0 copy-start.1
  0.7 0.0 copy-start.2
  0.7 0.0 copy-start.3
  0.7 2.8 %send_rows.1 = (bf16[768,256]{1,0:T(8,128)(2,1)}, bf16[768,256]{1,0:T(8,128)(2,1)}) custom-call(s32[3,48]{1,0:T(4,128)} %bitcast.9, s32[12]{0:T(128)} %up_hbm.1, s32[12]{0:T(128)} %down_hbm.1, s32[1]{0:T(128)} %bitcast.2.par, bf16[48,64,192]{2,1,0:T(8,128)(2,1)} %p_hbm.1), custom_call_target="tpu_custom_call" | custom-call | flops 20000000000 | bytes 1000000 | tf_op jit(solution)/shard_map/send_rows/pallas_call | solution.py:324
  3.5 0.1 collective-permute-start
  3.6 6.2 %collective-permute-start.1 = (bf16[768,256]{1,0:T(8,128)(2,1)}, bf16[768,256]{1,0:T(8,128)(2,1)S(1)}, u32[]{:S(2)}, u32[]{:S(2)}) collective-permute-start(bf16[768,256]{1,0:T(8,128)(2,1)} %get-tuple-element.22), channel_id=1, source_target_pairs={{4,8},{8,4},{12,16},{16,12},{20,24},{24,20},{28,32},{32,28},{36,40... | collective-permute-start | bytes 1179656 | tf_op jit(solution)/shard_map/ppermute | solution.py:307
  9.9 6.6 %own_columns.1 = (bf16[3072,256]{1,0:T(8,128)(2,1)S(1)}, bf16[512,3072]{1,0:T(8,128)(2,1)S(1)}, bf16[3072,256]{1,0:T(8,128)(2,1)S(1)}, bf16[3072,128]{1,0:T(8,12...) custom-call(s32[7,48]{1,0:T(8,128)S(1)} %bitcast.7, s32[3,48]{1,0:T(4,128)S(1)} %bitcast.10, ...), custom_call_target="tpu_custom_call" | custom-call | flops 4000000000 | bytes 20000000 | tf_op jit(solution)/shard_map/own_columns/pallas_call | solution.py:341
  16.6 0.0 collective-permute-done.got_a
  16.6 0.0 collective-permute-done.1.got_b
  16.6 5.7 %ghost_columns.1 = (bf16[272,768]{1,0:T(8,128)(2,1)S(1)}, bf16[272,768]{1,0:T(8,128)(2,1)S(1)}, bf16[30,3136,256]{2,1,0:T(8,128)(2,1)}) custom-call(s32[7,48]{1,0:T(8,128)S(1)} %bitcast.8, s32[128]{0:T(128)S(1)} %get-tuple-element.20.named, s32[1]{0:T(128)} %bitcast.2.par, bf16[768,256]{1,0:T(8,128)(2,1)S(1)} %collective-permute-done.got_a, ...), custom_call_target="tpu_custom_call" | custom-call | flops 3000000000 | bytes 1000000 | tf_op jit(solution)/shard_map/ghost_columns/pallas_call | solution.py:359
  22.3 0.1 collective-permute-start.2
  22.4 4.7 %collective-permute-start.3 = (bf16[272,768]{1,0:T(8,128)(2,1)S(1)}, bf16[272,768]{1,0:T(8,128)(2,1)S(1)}, u32[]{:S(2)}, u32[]{:S(2)}) collective-permute-start(bf16[272,768]{1,0:T(8,128)(2,1)S(1)} %get-tuple-element.29), channel_id=1, source_target_pairs={{4,8},{8,4},{12,16},{16,12},{20,24},{24,20},{28,32},{32,28},{36,40... | collective-permute-start | bytes 1253384 | tf_op jit(solution)/shard_map/ppermute | solution.py:307
  27.1 0.0 copy-start
  27.1 4.5 %home_rows.1 = (f32[256,768]{1,0:T(8,128)S(1)}, f32[16,256]{1,0:T(8,128)S(1)}) custom-call(bf16[30,3136,256]{2,1,0:T(8,128)(2,1)} %get-tuple-element.30.stash, bf16[3072,256]{1,0:T(8,128)(2,1)S(1)} %get-tuple-element.31.ap_ref), custom_call_target="tpu_custom_call" | custom-call | flops 3000000000 | bytes 1000000 | tf_op jit(solution)/shard_map/home_rows/pallas_call | solution.py:374
  31.6 0.0 collective-permute-done.2.got_a
  31.6 2.3 %collective-permute-done.3.got_b = bf16[272,768]{1,0:T(8,128)(2,1)S(1)} collective-permute-done((bf16[272,768]{1,0:T(8,128)(2,1)S(1)}, bf16[272,768]{1,0:T(8,128)(2,1)S(1)}, u32[]{:S(2)}, u32[]{:S(2)}) %collective-permute-start.3) | collective-permute-done | bytes 417824 | tf_op jit(solution)/shard_map/ppermute | solution.py:307
  33.9 0.9 %sum_rows.1 = (bf16[64,2688]{1,0:T(8,128)(2,1)S(1)}, bf16[64,2688]{1,0:T(8,128)(2,1)S(1)}, bf16[64,2688]{1,0:T(8,128)(2,1)S(1)}, bf16[64,2688]{1,0:T(8,128)(2,1)S(1)}) custom-call(s32[1,4]{1,0:T(1,128)S(1)} %bitcast.6, s32[1]{0:T(128)} %bitcast.2.par, s32[1]{0:T(128)} %bitcast.comp, bf16[272,768]{1,0:T(8,128)(2,1)S(1)} %collective-permute-done.2.got_a, ...), custom_call_target="tpu_custom_call" | custom-call | tf_op jit(solution)/shard_map/sum_rows/pallas_call | solution.py:389
  34.8 1.6 %collective-permute-start.4 = (bf16[64,2688]{1,0:T(8,128)(2,1)S(1)}, bf16[64,2688]{1,0:T(8,128)(2,1)S(1)}, u32[]{:S(2)}, u32[]{:S(2)}) collective-permute-start(bf16[64,2688]{1,0:T(8,128)(2,1)S(1)} %get-tuple-element.35), channel_id=1, source_target_pairs={{0,1},{1,2},{2,3},{3,0},{4,5},{5,6},{6,7},{7,4},{8,9},{9,10},{10,1... | collective-permute-start | bytes 1032200 | tf_op jit(solution)/shard_map/ppermute | solution.py:400
  36.3 1.7 %collective-permute-start.5 = (bf16[64,2688]{1,0:T(8,128)(2,1)S(1)}, bf16[64,2688]{1,0:T(8,128)(2,1)S(1)}, u32[]{:S(2)}, u32[]{:S(2)}) collective-permute-start(bf16[64,2688]{1,0:T(8,128)(2,1)S(1)} %get-tuple-element.36), channel_id=1, source_target_pairs={{0,2},{1,3},{2,0},{3,1},{4,6},{5,7},{6,4},{7,5},{8,10},{9,11},{10,... | collective-permute-start | bytes 1032200 | tf_op jit(solution)/shard_map/ppermute | solution.py:400
  38.1 2.4 %collective-permute-start.6 = (bf16[64,2688]{1,0:T(8,128)(2,1)S(1)}, bf16[64,2688]{1,0:T(8,128)(2,1)S(1)}, u32[]{:S(2)}, u32[]{:S(2)}) collective-permute-start(bf16[64,2688]{1,0:T(8,128)(2,1)S(1)} %get-tuple-element.37), channel_id=1, source_target_pairs={{0,3},{1,0},{2,1},{3,2},{4,7},{5,4},{6,5},{7,6},{8,11},{9,8},{10,9... | collective-permute-start | bytes 1032200 | tf_op jit(solution)/shard_map/ppermute | solution.py:400
  40.5 6.4 %collective-permute-done.4.refs_1_ = bf16[64,2688]{1,0:T(8,128)(2,1)S(1)} collective-permute-done((bf16[64,2688]{1,0:T(8,128)(2,1)S(1)}, bf16[64,2688]{1,0:T(8,128)(2,1)S(1)}, u32[]{:S(2)}, u32[]{:S(2)}) %collective-permute-start.4) | collective-permute-done | bytes 344096 | tf_op jit(solution)/shard_map/ppermute | solution.py:400
  46.9 5.3 %collective-permute-done.5.refs_2_ = bf16[64,2688]{1,0:T(8,128)(2,1)S(1)} collective-permute-done((bf16[64,2688]{1,0:T(8,128)(2,1)S(1)}, bf16[64,2688]{1,0:T(8,128)(2,1)S(1)}, u32[]{:S(2)}, u32[]{:S(2)}) %collective-permute-start.5) | collective-permute-done | bytes 344096 | tf_op jit(solution)/shard_map/ppermute | solution.py:400
  52.1 0.5 %collective-permute-done.6.refs_3_ = bf16[64,2688]{1,0:T(8,128)(2,1)S(1)} collective-permute-done((bf16[64,2688]{1,0:T(8,128)(2,1)S(1)}, bf16[64,2688]{1,0:T(8,128)(2,1)S(1)}, u32[]{:S(2)}, u32[]{:S(2)}) %collective-permute-start.6) | collective-permute-done | bytes 344096 | tf_op jit(solution)/shard_map/ppermute | solution.py:400
  52.7 1.1 %into_slots.1 = (bf16[8,64,1280]{2,1,0:T(8,128)(2,1)}, bf16[8,128]{1,0:T(8,128)(2,1)}) custom-call(s32[1]{0:T(128)} %bitcast.comp, bf16[64,2688]{1,0:T(8,128)(2,1)S(1)} %get-tuple-element.34.refs_0_, bf16[64,2688]{1,0:T(8,128)(2,1)S(1)} %collective-permute-done.4.refs_1_, bf16[64,2688]{1,0:T(8,128)(2,1)S(1)} %collective-permute-done.5.refs_2_, ...), custom_call_target="tpu_custom_call" | custom-call | tf_op jit(solution)/shard_map/into_slots/pallas_call | solution.py:401
  (12 shorter events, 0.0 us)
Async XLA Ops:
  0.6 9.2 %copy-start.1 = (bf16[48,64,448]{2,1,0:T(8,128)(2,1)S(1)}, bf16[48,64,448]{2,1,0:T(8,128)(2,1)}, u32[]{:S(2)}) copy-start(bf16[48,64,448]{2,1,0:T(8,128)(2,1)} %a_v.3) | copy-start | bytes 8257540
  0.7 9.2 %copy-start.2 = (bf16[48,64,192]{2,1,0:T(8,128)(2,1)S(1)}, bf16[48,64,192]{2,1,0:T(8,128)(2,1)}, u32[]{:S(2)}) copy-start(bf16[48,64,192]{2,1,0:T(8,128)(2,1)} %p_hbm.1) | copy-start | bytes 3538948
  0.7 9.2 %copy-start.3 = (bf16[48,64,192]{2,1,0:T(8,128)(2,1)S(1)}, bf16[48,64,192]{2,1,0:T(8,128)(2,1)}, u32[]{:S(2)}) copy-start(bf16[48,64,192]{2,1,0:T(8,128)(2,1)} %r_v.1) | copy-start | bytes 3538948
  0.7 9.2 %copy-start.4 = (bf16[48,128]{1,0:T(8,128)(2,1)S(1)}, bf16[48,128]{1,0:T(8,128)(2,1)}, u32[]{:S(2)}) copy-start(bf16[48,128]{1,0:T(8,128)(2,1)} %v_ref.1) | copy-start | bytes 36868
  0.7 9.2 %copy-start.5 = (s32[48,7]{0,1:T(8,128)S(1)}, s32[48,7]{0,1:T(8,128)}, u32[]{:S(2)}) copy-start(s32[48,7]{0,1:T(8,128)} %param.11) | copy-start | bytes 4036
  0.7 9.2 %copy-start.6 = (s32[48,3]{0,1:T(4,128)S(1)}, s32[48,3]{0,1:T(4,128)}, u32[]{:S(2)}) copy-start(s32[48,3]{0,1:T(4,128)} %param.13) | copy-start | bytes 1732
  0.7 9.2 %copy-start.7 = (s32[48,3]{0,1:T(4,128)S(1)}, s32[48,3]{0,1:T(4,128)}, u32[]{:S(2)}) copy-start(s32[48,3]{0,1:T(4,128)} %param.15) | copy-start | bytes 1732
  3.5 13.0 %collective-permute-start = (bf16[768,256]{1,0:T(8,128)(2,1)}, bf16[768,256]{1,0:T(8,128)(2,1)S(1)}, u32[]{:S(2)}, u32[]{:S(2)}) collective-permute-start(bf16[768,256]{1,0:T(8,128)(2,1)} %get-tuple-element.21), channel_id=1, source_target_pairs={{0,4},{4,0},{8,12},{12,8},{16,20},{20,16},{24,28},{28,24},{32,36},... | collective-permute-start | bytes 1179656 | tf_op jit(solution)/shard_map/ppermute | solution.py:312
  3.6 12.9 %collective-permute-start.1 = (bf16[768,256]{1,0:T(8,128)(2,1)}, bf16[768,256]{1,0:T(8,128)(2,1)S(1)}, u32[]{:S(2)}, u32[]{:S(2)}) collective-permute-start(bf16[768,256]{1,0:T(8,128)(2,1)} %get-tuple-element.22), channel_id=1, source_target_pairs={{4,8},{8,4},{12,16},{16,12},{20,24},{24,20},{28,32},{32,28},{36,40... | collective-permute-start | bytes 1179656 | tf_op jit(solution)/shard_map/ppermute | solution.py:307
  22.3 9.3 %collective-permute-start.2 = (bf16[272,768]{1,0:T(8,128)(2,1)S(1)}, bf16[272,768]{1,0:T(8,128)(2,1)S(1)}, u32[]{:S(2)}, u32[]{:S(2)}) collective-permute-start(bf16[272,768]{1,0:T(8,128)(2,1)S(1)} %get-tuple-element.28), channel_id=1, source_target_pairs={{0,4},{4,0},{8,12},{12,8},{16,20},{20,16},{24,28},{28,24},{32,36},... | collective-permute-start | bytes 1253384 | tf_op jit(solution)/shard_map/ppermute | solution.py:312
  22.4 11.5 %collective-permute-start.3 = (bf16[272,768]{1,0:T(8,128)(2,1)S(1)}, bf16[272,768]{1,0:T(8,128)(2,1)S(1)}, u32[]{:S(2)}, u32[]{:S(2)}) collective-permute-start(bf16[272,768]{1,0:T(8,128)(2,1)S(1)} %get-tuple-element.29), channel_id=1, source_target_pairs={{4,8},{8,4},{12,16},{16,12},{20,24},{24,20},{28,32},{32,28},{36,40... | collective-permute-start | bytes 1253384 | tf_op jit(solution)/shard_map/ppermute | solution.py:307
  27.1 6.8 %copy-start = (s32[4,1]{0,1:T(1,128)S(1)}, s32[4,1]{0,1:T(1,128)}, u32[]{:S(2)}) copy-start(s32[4,1]{0,1:T(1,128)} %param.19) | copy-start | bytes 52
  34.8 12.1 %collective-permute-start.4 = (bf16[64,2688]{1,0:T(8,128)(2,1)S(1)}, bf16[64,2688]{1,0:T(8,128)(2,1)S(1)}, u32[]{:S(2)}, u32[]{:S(2)}) collective-permute-start(bf16[64,2688]{1,0:T(8,128)(2,1)S(1)} %get-tuple-element.35), channel_id=1, source_target_pairs={{0,1},{1,2},{2,3},{3,0},{4,5},{5,6},{6,7},{7,4},{8,9},{9,10},{10,1... | collective-permute-start | bytes 1032200 | tf_op jit(solution)/shard_map/ppermute | solution.py:400
  36.3 15.8 %collective-permute-start.5 = (bf16[64,2688]{1,0:T(8,128)(2,1)S(1)}, bf16[64,2688]{1,0:T(8,128)(2,1)S(1)}, u32[]{:S(2)}, u32[]{:S(2)}) collective-permute-start(bf16[64,2688]{1,0:T(8,128)(2,1)S(1)} %get-tuple-element.36), channel_id=1, source_target_pairs={{0,2},{1,3},{2,0},{3,1},{4,6},{5,7},{6,4},{7,5},{8,10},{9,11},{10,... | collective-permute-start | bytes 1032200 | tf_op jit(solution)/shard_map/ppermute | solution.py:400
  38.1 14.6 %collective-permute-start.6 = (bf16[64,2688]{1,0:T(8,128)(2,1)S(1)}, bf16[64,2688]{1,0:T(8,128)(2,1)S(1)}, u32[]{:S(2)}, u32[]{:S(2)}) collective-permute-start(bf16[64,2688]{1,0:T(8,128)(2,1)S(1)} %get-tuple-element.37), channel_id=1, source_target_pairs={{0,3},{1,0},{2,1},{3,2},{4,7},{5,4},{6,5},{7,6},{8,11},{9,8},{10,9... | collective-permute-start | bytes 1032200 | tf_op jit(solution)/shard_map/ppermute | solution.py:400

commit v5 on v4

--- a/solution.py
+++ b/solution.py
@@ -14,6 +14,7 @@
 K1_FLOPS = 20 * 10**9
 K2_MIB = 24
 STASH = 30
+ORDER = (0, 2, 1, 3)
 K3_FLOPS = 3 * 10**9
 K4_FLOPS = 3 * 10**9
 
@@ -152,7 +153,7 @@
 
 
 def ghost_kernel(
-    acol, named, par, got_a, got_b, a_v, rd_ref, home_ref, mid_ref, vec_ref, spread_ref, send_a, send_b, stash, strips, table, sems, *, coarse
+    acol, named, par, got_b, got_a, a_v, rd_ref, home_ref, mid_ref, vec_ref, spread_ref, send_a, send_b, stash, strips, table, sems, *, coarse
 ):
     rows, width = a_v.shape[0], a_v.shape[1]
     kas = acol.shape[0]
@@ -231,7 +232,7 @@
     out_vec[...] = vec
 
 
-def sum_kernel(dest, par, comp, got_a, got_b, own, own_vec, *outs, coarse):
+def sum_kernel(dest, par, comp, got_b, got_a, own, own_vec, *outs, coarse):
     seg = own.shape[0]
     width = seg // coarse
     odd = par[0] == 1
@@ -293,7 +294,7 @@
     wide = matrix.shape[2]
     row = lax.broadcasted_iota(jnp.int32, (8, 128), 0)
     total = jnp.zeros((8, 128), F32)
-    for distance, part in enumerate(parts):
+    for distance, part in zip(ORDER, parts):
         source = lax.rem(comp[0] - distance + 4, 4)
         lines = part[0:16, 2 * wide :].astype(F32)
         for k in range(2):
@@ -369,7 +370,7 @@
         compiler_params=params(K2_MIB),
         cost_estimate=pl.CostEstimate(flops=K3_FLOPS, bytes_accessed=10**6, transcendentals=0),
         name="ghost_columns",
-    )(acol, named, par, got_a, got_b, a_blocks, sides_dense, home_dense, mid, side_vec, spread)
+    )(acol, named, par, got_b, got_a, a_blocks, sides_dense, home_dense, mid, side_vec, spread)
     from_b, from_a = across(send_b), within(send_a)
     own, own_vec = pl.pallas_call(
         home_kernel,
@@ -393,7 +394,7 @@
         out_specs=[VM] * 4,
         compiler_params=params(),
         name="sum_rows",
-    )(dest, par, comp, from_a, from_b, own, own_vec)
+    )(dest, par, comp, from_b, from_a, own, own_vec)
     parts = [outs[0]]
     turned = {}
     for distance in (2, 1, 3):
@@ -405,7 +406,7 @@
         out_specs=[VM, VM],
         compiler_params=params(),
         name="into_slots",
-    )(comp, outs[0], turned[1], turned[2], turned[3])
+    )(comp, outs[0], *[turned[distance] for distance in ORDER[1:]])
 
 
 def solution(mesh):

time: 54.3 us -> 53.1 us (0.978)
  starting transfers between devices: 16.8 us -> 15.6 us
    ppermute x2, starting transfers between devices: 10.9 us -> 10.1 us  [across(): lax.ppermute(block, 'mesh', [(i, i + 1 if i % 2 else i - 1) for i in rang...]
where the time goes in v5:
time: 53.1 us; the launch traced here: 52.9 us
  Pallas kernels  21.7 us (41%)
  starting transfers between devices  15.6 us (29%)
  waiting for transfers between devices  14.7 us (28%)
  between operations  0.86 us (2%)
    ppermute x3, waiting for transfers between devices, on_device(): lax.ppermute(outs[distance], 'comp', [(i, (i + distance) % 4) for i in ra...  12.4 us
    ppermute x2, starting transfers between devices, across(): lax.ppermute(block, 'mesh', [(i, i + 1 if i % 2 else i - 1) for i in rang...  10.1 us
    pallas_call x1, Pallas kernels, on_device(): pl.pallas_call(functools.partial(own_kernel, coarse=coarse), out_shape=[s...  6.63 us
    pallas_call x1, Pallas kernels, on_device(): pl.pallas_call(functools.partial(ghost_kernel, coarse=coarse), out_shape=...  5.71 us
    ppermute x3, starting transfers between devices, on_device(): lax.ppermute(outs[distance], 'comp', [(i, (i + distance) % 4) for i in ra...  5.33 us
    pallas_call x1, Pallas kernels, on_device(): pl.pallas_call(home_kernel, out_shape=[shape((seg, 3 * seg), F32), shape(...  4.48 us
    pallas_call x1, Pallas kernels, on_device(): pl.pallas_call(functools.partial(send_kernel, coarse=coarse), out_shape=[...  2.82 us
    ppermute x2, waiting for transfers between devices, across(): lax.ppermute(block, 'mesh', [(i, i + 1 if i % 2 else i - 1) for i in rang...  2.29 us
  transfers between devices with their start and end apart: 7, of which 4 were waited for; matrix products, arithmetic and copies ran while one was open for 0% of the time, Pallas kernels for 21%

profile of v5, /device:TPU:24, one launch (start us, length us, event | category | flops | bytes accessed | tf_op | source)
XLA Modules:
  0.0 52.9 jit_solution(13251305344551919623)
XLA Ops:
  0.6 0.0 copy-start.1
  0.7 0.0 copy-start.2
  0.7 0.0 copy-start.3
  0.7 2.8 %send_rows.1 = (bf16[768,256]{1,0:T(8,128)(2,1)}, bf16[768,256]{1,0:T(8,128)(2,1)}) custom-call(s32[3,48]{1,0:T(4,128)} %bitcast.9, s32[12]{0:T(128)} %up_hbm.1, s32[12]{0:T(128)} %down_hbm.1, s32[1]{0:T(128)} %bitcast.2.par, bf16[48,64,192]{2,1,0:T(8,128)(2,1)} %p_hbm.1), custom_call_target="tpu_custom_call" | custom-call | flops 20000000000 | bytes 1000000 | tf_op jit(solution)/shard_map/send_rows/pallas_call | solution.py:325
  3.5 5.6 %collective-permute-start = (bf16[768,256]{1,0:T(8,128)(2,1)}, bf16[768,256]{1,0:T(8,128)(2,1)S(1)}, u32[]{:S(2)}, u32[]{:S(2)}) collective-permute-start(bf16[768,256]{1,0:T(8,128)(2,1)} %get-tuple-element.21), channel_id=1, source_target_pairs={{4,8},{8,4},{12,16},{16,12},{20,24},{24,20},{28,32},{32,28},{36,40... | collective-permute-start | bytes 1179656 | tf_op jit(solution)/shard_map/ppermute | solution.py:308
  9.1 0.1 collective-permute-start.1
  9.3 6.6 %own_columns.1 = (bf16[3072,256]{1,0:T(8,128)(2,1)S(1)}, bf16[512,3072]{1,0:T(8,128)(2,1)S(1)}, bf16[3072,256]{1,0:T(8,128)(2,1)S(1)}, bf16[3072,128]{1,0:T(8,12...) custom-call(s32[7,48]{1,0:T(8,128)S(1)} %bitcast.7, s32[3,48]{1,0:T(4,128)S(1)} %bitcast.10, ...), custom_call_target="tpu_custom_call" | custom-call | flops 4000000000 | bytes 20000000 | tf_op jit(solution)/shard_map/own_columns/pallas_call | solution.py:342
  15.9 0.0 collective-permute-done.got_b
  15.9 0.0 collective-permute-done.1.got_a
  15.9 5.7 %ghost_columns.1 = (bf16[272,768]{1,0:T(8,128)(2,1)S(1)}, bf16[272,768]{1,0:T(8,128)(2,1)S(1)}, bf16[30,3136,256]{2,1,0:T(8,128)(2,1)}) custom-call(s32[7,48]{1,0:T(8,128)S(1)} %bitcast.8, s32[128]{0:T(128)S(1)} %get-tuple-element.20.named, s32[1]{0:T(128)} %bitcast.2.par, bf16[768,256]{1,0:T(8,128)(2,1)S(1)} %collective-permute-done.got_b, ...), custom_call_target="tpu_custom_call" | custom-call | flops 3000000000 | bytes 1000000 | tf_op jit(solution)/shard_map/ghost_columns/pallas_call | solution.py:360
  21.6 4.6 %collective-permute-start.2 = (bf16[272,768]{1,0:T(8,128)(2,1)S(1)}, bf16[272,768]{1,0:T(8,128)(2,1)S(1)}, u32[]{:S(2)}, u32[]{:S(2)}) collective-permute-start(bf16[272,768]{1,0:T(8,128)(2,1)S(1)} %get-tuple-element.28), channel_id=1, source_target_pairs={{4,8},{8,4},{12,16},{16,12},{20,24},{24,20},{28,32},{32,28},{36,40... | collective-permute-start | bytes 1253384 | tf_op jit(solution)/shard_map/ppermute | solution.py:308
  26.2 0.1 collective-permute-start.3
  26.3 0.0 copy-start
  26.3 4.5 %home_rows.1 = (f32[256,768]{1,0:T(8,128)S(1)}, f32[16,256]{1,0:T(8,128)S(1)}) custom-call(bf16[30,3136,256]{2,1,0:T(8,128)(2,1)} %get-tuple-element.30.stash, bf16[3072,256]{1,0:T(8,128)(2,1)S(1)} %get-tuple-element.31.ap_ref), custom_call_target="tpu_custom_call" | custom-call | flops 3000000000 | bytes 1000000 | tf_op jit(solution)/shard_map/home_rows/pallas_call | solution.py:375
  30.8 2.3 %collective-permute-done.2.got_b = bf16[272,768]{1,0:T(8,128)(2,1)S(1)} collective-permute-done((bf16[272,768]{1,0:T(8,128)(2,1)S(1)}, bf16[272,768]{1,0:T(8,128)(2,1)S(1)}, u32[]{:S(2)}, u32[]{:S(2)}) %collective-permute-start.2) | collective-permute-done | bytes 417824 | tf_op jit(solution)/shard_map/ppermute | solution.py:308
  33.1 0.0 collective-permute-done.3.got_a
  33.1 0.9 %sum_rows.1 = (bf16[64,2688]{1,0:T(8,128)(2,1)S(1)}, bf16[64,2688]{1,0:T(8,128)(2,1)S(1)}, bf16[64,2688]{1,0:T(8,128)(2,1)S(1)}, bf16[64,2688]{1,0:T(8,128)(2,1)S(1)}) custom-call(s32[1,4]{1,0:T(1,128)S(1)} %bitcast.6, s32[1]{0:T(128)} %bitcast.2.par, s32[1]{0:T(128)} %bitcast.comp, bf16[272,768]{1,0:T(8,128)(2,1)S(1)} %collective-permute-done.2.got_b, ...), custom_call_target="tpu_custom_call" | custom-call | tf_op jit(solution)/shard_map/sum_rows/pallas_call | solution.py:390
  34.0 2.1 %collective-permute-start.4 = (bf16[64,2688]{1,0:T(8,128)(2,1)S(1)}, bf16[64,2688]{1,0:T(8,128)(2,1)S(1)}, u32[]{:S(2)}, u32[]{:S(2)}) collective-permute-start(bf16[64,2688]{1,0:T(8,128)(2,1)S(1)} %get-tuple-element.35), channel_id=1, source_target_pairs={{0,2},{1,3},{2,0},{3,1},{4,6},{5,7},{6,4},{7,5},{8,10},{9,11},{10,... | collective-permute-start | bytes 1032200 | tf_op jit(solution)/shard_map/ppermute | solution.py:401
  36.1 1.6 %collective-permute-start.5 = (bf16[64,2688]{1,0:T(8,128)(2,1)S(1)}, bf16[64,2688]{1,0:T(8,128)(2,1)S(1)}, u32[]{:S(2)}, u32[]{:S(2)}) collective-permute-start(bf16[64,2688]{1,0:T(8,128)(2,1)S(1)} %get-tuple-element.36), channel_id=1, source_target_pairs={{0,1},{1,2},{2,3},{3,0},{4,5},{5,6},{6,7},{7,4},{8,9},{9,10},{10,1... | collective-permute-start | bytes 1032200 | tf_op jit(solution)/shard_map/ppermute | solution.py:401
  37.7 1.6 %collective-permute-start.6 = (bf16[64,2688]{1,0:T(8,128)(2,1)S(1)}, bf16[64,2688]{1,0:T(8,128)(2,1)S(1)}, u32[]{:S(2)}, u32[]{:S(2)}) collective-permute-start(bf16[64,2688]{1,0:T(8,128)(2,1)S(1)} %get-tuple-element.37), channel_id=1, source_target_pairs={{0,3},{1,0},{2,1},{3,2},{4,7},{5,4},{6,5},{7,6},{8,11},{9,8},{10,9... | collective-permute-start | bytes 1032200 | tf_op jit(solution)/shard_map/ppermute | solution.py:401
  39.4 7.3 %collective-permute-done.4.refs_1_ = bf16[64,2688]{1,0:T(8,128)(2,1)S(1)} collective-permute-done((bf16[64,2688]{1,0:T(8,128)(2,1)S(1)}, bf16[64,2688]{1,0:T(8,128)(2,1)S(1)}, u32[]{:S(2)}, u32[]{:S(2)}) %collective-permute-start.4) | collective-permute-done | bytes 344096 | tf_op jit(solution)/shard_map/ppermute | solution.py:401
  46.7 5.0 %collective-permute-done.5.refs_2_ = bf16[64,2688]{1,0:T(8,128)(2,1)S(1)} collective-permute-done((bf16[64,2688]{1,0:T(8,128)(2,1)S(1)}, bf16[64,2688]{1,0:T(8,128)(2,1)S(1)}, u32[]{:S(2)}, u32[]{:S(2)}) %collective-permute-start.5) | collective-permute-done | bytes 344096 | tf_op jit(solution)/shard_map/ppermute | solution.py:401
  51.6 0.1 collective-permute-done.6.refs_3_
  51.7 1.1 %into_slots.1 = (bf16[8,64,1280]{2,1,0:T(8,128)(2,1)}, bf16[8,128]{1,0:T(8,128)(2,1)}) custom-call(s32[1]{0:T(128)} %bitcast.comp, bf16[64,2688]{1,0:T(8,128)(2,1)S(1)} %get-tuple-element.34.refs_0_, bf16[64,2688]{1,0:T(8,128)(2,1)S(1)} %collective-permute-done.4.refs_1_, bf16[64,2688]{1,0:T(8,128)(2,1)S(1)} %collective-permute-done.5.refs_2_, ...), custom_call_target="tpu_custom_call" | custom-call | tf_op jit(solution)/shard_map/into_slots/pallas_call | solution.py:402
  (12 shorter events, 0.0 us)
Async XLA Ops:
  0.6 8.6 %copy-start.1 = (bf16[48,64,448]{2,1,0:T(8,128)(2,1)S(1)}, bf16[48,64,448]{2,1,0:T(8,128)(2,1)}, u32[]{:S(2)}) copy-start(bf16[48,64,448]{2,1,0:T(8,128)(2,1)} %a_v.3) | copy-start | bytes 8257540
  0.7 8.6 %copy-start.2 = (bf16[48,64,192]{2,1,0:T(8,128)(2,1)S(1)}, bf16[48,64,192]{2,1,0:T(8,128)(2,1)}, u32[]{:S(2)}) copy-start(bf16[48,64,192]{2,1,0:T(8,128)(2,1)} %p_hbm.1) | copy-start | bytes 3538948
  0.7 8.6 %copy-start.3 = (bf16[48,64,192]{2,1,0:T(8,128)(2,1)S(1)}, bf16[48,64,192]{2,1,0:T(8,128)(2,1)}, u32[]{:S(2)}) copy-start(bf16[48,64,192]{2,1,0:T(8,128)(2,1)} %r_v.1) | copy-start | bytes 3538948
  0.7 8.6 %copy-start.4 = (bf16[48,128]{1,0:T(8,128)(2,1)S(1)}, bf16[48,128]{1,0:T(8,128)(2,1)}, u32[]{:S(2)}) copy-start(bf16[48,128]{1,0:T(8,128)(2,1)} %v_ref.1) | copy-start | bytes 36868
  0.7 8.6 %copy-start.5 = (s32[48,7]{0,1:T(8,128)S(1)}, s32[48,7]{0,1:T(8,128)}, u32[]{:S(2)}) copy-start(s32[48,7]{0,1:T(8,128)} %param.11) | copy-start | bytes 4036
  0.7 8.6 %copy-start.6 = (s32[48,3]{0,1:T(4,128)S(1)}, s32[48,3]{0,1:T(4,128)}, u32[]{:S(2)}) copy-start(s32[48,3]{0,1:T(4,128)} %param.13) | copy-start | bytes 1732
  0.7 8.6 %copy-start.7 = (s32[48,3]{0,1:T(4,128)S(1)}, s32[48,3]{0,1:T(4,128)}, u32[]{:S(2)}) copy-start(s32[48,3]{0,1:T(4,128)} %param.15) | copy-start | bytes 1732
  3.5 12.4 %collective-permute-start = (bf16[768,256]{1,0:T(8,128)(2,1)}, bf16[768,256]{1,0:T(8,128)(2,1)S(1)}, u32[]{:S(2)}, u32[]{:S(2)}) collective-permute-start(bf16[768,256]{1,0:T(8,128)(2,1)} %get-tuple-element.21), channel_id=1, source_target_pairs={{4,8},{8,4},{12,16},{16,12},{20,24},{24,20},{28,32},{32,28},{36,40... | collective-permute-start | bytes 1179656 | tf_op jit(solution)/shard_map/ppermute | solution.py:308
  9.1 6.8 %collective-permute-start.1 = (bf16[768,256]{1,0:T(8,128)(2,1)}, bf16[768,256]{1,0:T(8,128)(2,1)S(1)}, u32[]{:S(2)}, u32[]{:S(2)}) collective-permute-start(bf16[768,256]{1,0:T(8,128)(2,1)} %get-tuple-element.22), channel_id=1, source_target_pairs={{0,4},{4,0},{8,12},{12,8},{16,20},{20,16},{24,28},{28,24},{32,36},... | collective-permute-start | bytes 1179656 | tf_op jit(solution)/shard_map/ppermute | solution.py:313
  21.6 11.5 %collective-permute-start.2 = (bf16[272,768]{1,0:T(8,128)(2,1)S(1)}, bf16[272,768]{1,0:T(8,128)(2,1)S(1)}, u32[]{:S(2)}, u32[]{:S(2)}) collective-permute-start(bf16[272,768]{1,0:T(8,128)(2,1)S(1)} %get-tuple-element.28), channel_id=1, source_target_pairs={{4,8},{8,4},{12,16},{16,12},{20,24},{24,20},{28,32},{32,28},{36,40... | collective-permute-start | bytes 1253384 | tf_op jit(solution)/shard_map/ppermute | solution.py:308
  26.2 6.9 %collective-permute-start.3 = (bf16[272,768]{1,0:T(8,128)(2,1)S(1)}, bf16[272,768]{1,0:T(8,128)(2,1)S(1)}, u32[]{:S(2)}, u32[]{:S(2)}) collective-permute-start(bf16[272,768]{1,0:T(8,128)(2,1)S(1)} %get-tuple-element.29), channel_id=1, source_target_pairs={{0,4},{4,0},{8,12},{12,8},{16,20},{20,16},{24,28},{28,24},{32,36},... | collective-permute-start | bytes 1253384 | tf_op jit(solution)/shard_map/ppermute | solution.py:313
  26.3 6.8 %copy-start = (s32[4,1]{0,1:T(1,128)S(1)}, s32[4,1]{0,1:T(1,128)}, u32[]{:S(2)}) copy-start(s32[4,1]{0,1:T(1,128)} %param.19) | copy-start | bytes 52
  34.0 12.6 %collective-permute-start.4 = (bf16[64,2688]{1,0:T(8,128)(2,1)S(1)}, bf16[64,2688]{1,0:T(8,128)(2,1)S(1)}, u32[]{:S(2)}, u32[]{:S(2)}) collective-permute-start(bf16[64,2688]{1,0:T(8,128)(2,1)S(1)} %get-tuple-element.35), channel_id=1, source_target_pairs={{0,2},{1,3},{2,0},{3,1},{4,6},{5,7},{6,4},{7,5},{8,10},{9,11},{10,... | collective-permute-start | bytes 1032200 | tf_op jit(solution)/shard_map/ppermute | solution.py:401
  36.1 15.5 %collective-permute-start.5 = (bf16[64,2688]{1,0:T(8,128)(2,1)S(1)}, bf16[64,2688]{1,0:T(8,128)(2,1)S(1)}, u32[]{:S(2)}, u32[]{:S(2)}) collective-permute-start(bf16[64,2688]{1,0:T(8,128)(2,1)S(1)} %get-tuple-element.36), channel_id=1, source_target_pairs={{0,1},{1,2},{2,3},{3,0},{4,5},{5,6},{6,7},{7,4},{8,9},{9,10},{10,1... | collective-permute-start | bytes 1032200 | tf_op jit(solution)/shard_map/ppermute | solution.py:401
  37.7 14.0 %collective-permute-start.6 = (bf16[64,2688]{1,0:T(8,128)(2,1)S(1)}, bf16[64,2688]{1,0:T(8,128)(2,1)S(1)}, u32[]{:S(2)}, u32[]{:S(2)}) collective-permute-start(bf16[64,2688]{1,0:T(8,128)(2,1)S(1)} %get-tuple-element.37), channel_id=1, source_target_pairs={{0,3},{1,0},{2,1},{3,2},{4,7},{5,4},{6,5},{7,6},{8,11},{9,8},{10,9... | collective-permute-start | bytes 1032200 | tf_op jit(solution)/shard_map/ppermute | solution.py:401

commit v6 on v5

--- a/solution.py
+++ b/solution.py
@@ -173,7 +173,7 @@
     table[2 * block :, :] = jnp.zeros((width, seg), BF)
     strips[...] = jnp.zeros_like(strips)
     count = named[127]
-    batch = 20
+    batch = 26
 
     def apply(n, _):
         for i in range(batch):

time: 53.1 us -> 52.9 us (level)
  starting transfers between devices: 15.6 us -> 16.6 us
  waiting for transfers between devices: 14.7 us -> 13.7 us
    ppermute x3, waiting for transfers between devices: 12.4 us -> 11.4 us  [on_device(): lax.ppermute(outs[distance], 'comp', [(i, (i + distance) % 4) for i in ra...]
    ppermute x3, starting transfers between devices: 5.33 us -> 6.33 us  [on_device(): lax.ppermute(outs[distance], 'comp', [(i, (i + distance) % 4) for i in ra...]
where the time goes in v6:
time: 52.9 us; the launch traced here: 52.4 us
  Pallas kernels  21.2 us (40%)
  starting transfers between devices  16.6 us (31%)
  waiting for transfers between devices  13.7 us (26%)
  between operations  0.86 us (2%)
    ppermute x3, waiting for transfers between devices, on_device(): lax.ppermute(outs[distance], 'comp', [(i, (i + distance) % 4) for i in ra...  11.4 us
    ppermute x2, starting transfers between devices, across(): lax.ppermute(block, 'mesh', [(i, i + 1 if i % 2 else i - 1) for i in rang...  10.1 us
    pallas_call x1, Pallas kernels, on_device(): pl.pallas_call(functools.partial(own_kernel, coarse=coarse), out_shape=[s...  6.63 us
    ppermute x3, starting transfers between devices, on_device(): lax.ppermute(outs[distance], 'comp', [(i, (i + distance) % 4) for i in ra...  6.33 us
    pallas_call x1, Pallas kernels, on_device(): pl.pallas_call(functools.partial(ghost_kernel, coarse=coarse), out_shape=...  5.23 us
    pallas_call x1, Pallas kernels, on_device(): pl.pallas_call(home_kernel, out_shape=[shape((seg, 3 * seg), F32), shape(...  4.48 us
    pallas_call x1, Pallas kernels, on_device(): pl.pallas_call(functools.partial(send_kernel, coarse=coarse), out_shape=[...  2.82 us
    ppermute x2, waiting for transfers between devices, across(): lax.ppermute(block, 'mesh', [(i, i + 1 if i % 2 else i - 1) for i in rang...  2.29 us
  transfers between devices with their start and end apart: 7, of which 4 were waited for; matrix products, arithmetic and copies ran while one was open for 0% of the time, Pallas kernels for 21%

profile of v6, /device:TPU:24, one launch (start us, length us, event | category | flops | bytes accessed | tf_op | source)
XLA Modules:
  0.0 52.4 jit_solution(11687695105659201425)
XLA Ops:
  0.6 0.0 copy-start.1
  0.7 0.0 copy-start.2
  0.7 0.0 copy-start.3
  0.7 2.8 %send_rows.1 = (bf16[768,256]{1,0:T(8,128)(2,1)}, bf16[768,256]{1,0:T(8,128)(2,1)}) custom-call(s32[3,48]{1,0:T(4,128)} %bitcast.9, s32[12]{0:T(128)} %up_hbm.1, s32[12]{0:T(128)} %down_hbm.1, s32[1]{0:T(128)} %bitcast.2.par, bf16[48,64,192]{2,1,0:T(8,128)(2,1)} %p_hbm.1), custom_call_target="tpu_custom_call" | custom-call | flops 20000000000 | bytes 1000000 | tf_op jit(solution)/shard_map/send_rows/pallas_call | solution.py:325
  3.5 5.6 %collective-permute-start = (bf16[768,256]{1,0:T(8,128)(2,1)}, bf16[768,256]{1,0:T(8,128)(2,1)S(1)}, u32[]{:S(2)}, u32[]{:S(2)}) collective-permute-start(bf16[768,256]{1,0:T(8,128)(2,1)} %get-tuple-element.21), channel_id=1, source_target_pairs={{4,8},{8,4},{12,16},{16,12},{20,24},{24,20},{28,32},{32,28},{36,40... | collective-permute-start | bytes 1179656 | tf_op jit(solution)/shard_map/ppermute | solution.py:308
  9.1 0.1 collective-permute-start.1
  9.3 6.6 %own_columns.1 = (bf16[3072,256]{1,0:T(8,128)(2,1)S(1)}, bf16[512,3072]{1,0:T(8,128)(2,1)S(1)}, bf16[3072,256]{1,0:T(8,128)(2,1)S(1)}, bf16[3072,128]{1,0:T(8,12...) custom-call(s32[7,48]{1,0:T(8,128)S(1)} %bitcast.7, s32[3,48]{1,0:T(4,128)S(1)} %bitcast.10, ...), custom_call_target="tpu_custom_call" | custom-call | flops 4000000000 | bytes 20000000 | tf_op jit(solution)/shard_map/own_columns/pallas_call | solution.py:342
  15.9 0.0 collective-permute-done.got_b
  15.9 0.0 collective-permute-done.1.got_a
  15.9 5.2 %ghost_columns.1 = (bf16[272,768]{1,0:T(8,128)(2,1)S(1)}, bf16[272,768]{1,0:T(8,128)(2,1)S(1)}, bf16[30,3136,256]{2,1,0:T(8,128)(2,1)}) custom-call(s32[7,48]{1,0:T(8,128)S(1)} %bitcast.8, s32[128]{0:T(128)S(1)} %get-tuple-element.20.named, s32[1]{0:T(128)} %bitcast.2.par, bf16[768,256]{1,0:T(8,128)(2,1)S(1)} %collective-permute-done.got_b, ...), custom_call_target="tpu_custom_call" | custom-call | flops 3000000000 | bytes 1000000 | tf_op jit(solution)/shard_map/ghost_columns/pallas_call | solution.py:360
  21.2 4.6 %collective-permute-start.2 = (bf16[272,768]{1,0:T(8,128)(2,1)S(1)}, bf16[272,768]{1,0:T(8,128)(2,1)S(1)}, u32[]{:S(2)}, u32[]{:S(2)}) collective-permute-start(bf16[272,768]{1,0:T(8,128)(2,1)S(1)} %get-tuple-element.28), channel_id=1, source_target_pairs={{4,8},{8,4},{12,16},{16,12},{20,24},{24,20},{28,32},{32,28},{36,40... | collective-permute-start | bytes 1253384 | tf_op jit(solution)/shard_map/ppermute | solution.py:308
  25.8 0.1 collective-permute-start.3
  25.8 0.0 copy-start
  25.9 4.5 %home_rows.1 = (f32[256,768]{1,0:T(8,128)S(1)}, f32[16,256]{1,0:T(8,128)S(1)}) custom-call(bf16[30,3136,256]{2,1,0:T(8,128)(2,1)} %get-tuple-element.30.stash, bf16[3072,256]{1,0:T(8,128)(2,1)S(1)} %get-tuple-element.31.ap_ref), custom_call_target="tpu_custom_call" | custom-call | flops 3000000000 | bytes 1000000 | tf_op jit(solution)/shard_map/home_rows/pallas_call | solution.py:375
  30.3 2.3 %collective-permute-done.2.got_b = bf16[272,768]{1,0:T(8,128)(2,1)S(1)} collective-permute-done((bf16[272,768]{1,0:T(8,128)(2,1)S(1)}, bf16[272,768]{1,0:T(8,128)(2,1)S(1)}, u32[]{:S(2)}, u32[]{:S(2)}) %collective-permute-start.2) | collective-permute-done | bytes 417824 | tf_op jit(solution)/shard_map/ppermute | solution.py:308
  32.6 0.0 collective-permute-done.3.got_a
  32.6 0.9 %sum_rows.1 = (bf16[64,2688]{1,0:T(8,128)(2,1)S(1)}, bf16[64,2688]{1,0:T(8,128)(2,1)S(1)}, bf16[64,2688]{1,0:T(8,128)(2,1)S(1)}, bf16[64,2688]{1,0:T(8,128)(2,1)S(1)}) custom-call(s32[1,4]{1,0:T(1,128)S(1)} %bitcast.6, s32[1]{0:T(128)} %bitcast.2.par, s32[1]{0:T(128)} %bitcast.comp, bf16[272,768]{1,0:T(8,128)(2,1)S(1)} %collective-permute-done.2.got_b, ...), custom_call_target="tpu_custom_call" | custom-call | tf_op jit(solution)/shard_map/sum_rows/pallas_call | solution.py:390
  33.6 3.1 %collective-permute-start.4 = (bf16[64,2688]{1,0:T(8,128)(2,1)S(1)}, bf16[64,2688]{1,0:T(8,128)(2,1)S(1)}, u32[]{:S(2)}, u32[]{:S(2)}) collective-permute-start(bf16[64,2688]{1,0:T(8,128)(2,1)S(1)} %get-tuple-element.35), channel_id=1, source_target_pairs={{0,2},{1,3},{2,0},{3,1},{4,6},{5,7},{6,4},{7,5},{8,10},{9,11},{10,... | collective-permute-start | bytes 1032200 | tf_op jit(solution)/shard_map/ppermute | solution.py:401
  36.7 0.6 %collective-permute-start.5 = (bf16[64,2688]{1,0:T(8,128)(2,1)S(1)}, bf16[64,2688]{1,0:T(8,128)(2,1)S(1)}, u32[]{:S(2)}, u32[]{:S(2)}) collective-permute-start(bf16[64,2688]{1,0:T(8,128)(2,1)S(1)} %get-tuple-element.36), channel_id=1, source_target_pairs={{0,1},{1,2},{2,3},{3,0},{4,5},{5,6},{6,7},{7,4},{8,9},{9,10},{10,1... | collective-permute-start | bytes 1032200 | tf_op jit(solution)/shard_map/ppermute | solution.py:401
  37.3 2.6 %collective-permute-start.6 = (bf16[64,2688]{1,0:T(8,128)(2,1)S(1)}, bf16[64,2688]{1,0:T(8,128)(2,1)S(1)}, u32[]{:S(2)}, u32[]{:S(2)}) collective-permute-start(bf16[64,2688]{1,0:T(8,128)(2,1)S(1)} %get-tuple-element.37), channel_id=1, source_target_pairs={{0,3},{1,0},{2,1},{3,2},{4,7},{5,4},{6,5},{7,6},{8,11},{9,8},{10,9... | collective-permute-start | bytes 1032200 | tf_op jit(solution)/shard_map/ppermute | solution.py:401
  39.9 6.3 %collective-permute-done.4.refs_1_ = bf16[64,2688]{1,0:T(8,128)(2,1)S(1)} collective-permute-done((bf16[64,2688]{1,0:T(8,128)(2,1)S(1)}, bf16[64,2688]{1,0:T(8,128)(2,1)S(1)}, u32[]{:S(2)}, u32[]{:S(2)}) %collective-permute-start.4) | collective-permute-done | bytes 344096 | tf_op jit(solution)/shard_map/ppermute | solution.py:401
  46.2 5.0 %collective-permute-done.5.refs_2_ = bf16[64,2688]{1,0:T(8,128)(2,1)S(1)} collective-permute-done((bf16[64,2688]{1,0:T(8,128)(2,1)S(1)}, bf16[64,2688]{1,0:T(8,128)(2,1)S(1)}, u32[]{:S(2)}, u32[]{:S(2)}) %collective-permute-start.5) | collective-permute-done | bytes 344096 | tf_op jit(solution)/shard_map/ppermute | solution.py:401
  51.1 0.1 collective-permute-done.6.refs_3_
  51.3 1.1 %into_slots.1 = (bf16[8,64,1280]{2,1,0:T(8,128)(2,1)}, bf16[8,128]{1,0:T(8,128)(2,1)}) custom-call(s32[1]{0:T(128)} %bitcast.comp, bf16[64,2688]{1,0:T(8,128)(2,1)S(1)} %get-tuple-element.34.refs_0_, bf16[64,2688]{1,0:T(8,128)(2,1)S(1)} %collective-permute-done.4.refs_1_, bf16[64,2688]{1,0:T(8,128)(2,1)S(1)} %collective-permute-done.5.refs_2_, ...), custom_call_target="tpu_custom_call" | custom-call | tf_op jit(solution)/shard_map/into_slots/pallas_call | solution.py:402
  (12 shorter events, 0.0 us)
Async XLA Ops:
  0.6 8.6 %copy-start.1 = (bf16[48,64,448]{2,1,0:T(8,128)(2,1)S(1)}, bf16[48,64,448]{2,1,0:T(8,128)(2,1)}, u32[]{:S(2)}) copy-start(bf16[48,64,448]{2,1,0:T(8,128)(2,1)} %a_v.3) | copy-start | bytes 8257540
  0.7 8.6 %copy-start.2 = (bf16[48,64,192]{2,1,0:T(8,128)(2,1)S(1)}, bf16[48,64,192]{2,1,0:T(8,128)(2,1)}, u32[]{:S(2)}) copy-start(bf16[48,64,192]{2,1,0:T(8,128)(2,1)} %p_hbm.1) | copy-start | bytes 3538948
  0.7 8.6 %copy-start.3 = (bf16[48,64,192]{2,1,0:T(8,128)(2,1)S(1)}, bf16[48,64,192]{2,1,0:T(8,128)(2,1)}, u32[]{:S(2)}) copy-start(bf16[48,64,192]{2,1,0:T(8,128)(2,1)} %r_v.1) | copy-start | bytes 3538948
  0.7 8.6 %copy-start.4 = (bf16[48,128]{1,0:T(8,128)(2,1)S(1)}, bf16[48,128]{1,0:T(8,128)(2,1)}, u32[]{:S(2)}) copy-start(bf16[48,128]{1,0:T(8,128)(2,1)} %v_ref.1) | copy-start | bytes 36868
  0.7 8.6 %copy-start.5 = (s32[48,7]{0,1:T(8,128)S(1)}, s32[48,7]{0,1:T(8,128)}, u32[]{:S(2)}) copy-start(s32[48,7]{0,1:T(8,128)} %param.11) | copy-start | bytes 4036
  0.7 8.6 %copy-start.6 = (s32[48,3]{0,1:T(4,128)S(1)}, s32[48,3]{0,1:T(4,128)}, u32[]{:S(2)}) copy-start(s32[48,3]{0,1:T(4,128)} %param.13) | copy-start | bytes 1732
  0.7 8.6 %copy-start.7 = (s32[48,3]{0,1:T(4,128)S(1)}, s32[48,3]{0,1:T(4,128)}, u32[]{:S(2)}) copy-start(s32[48,3]{0,1:T(4,128)} %param.15) | copy-start | bytes 1732
  3.5 12.4 %collective-permute-start = (bf16[768,256]{1,0:T(8,128)(2,1)}, bf16[768,256]{1,0:T(8,128)(2,1)S(1)}, u32[]{:S(2)}, u32[]{:S(2)}) collective-permute-start(bf16[768,256]{1,0:T(8,128)(2,1)} %get-tuple-element.21), channel_id=1, source_target_pairs={{4,8},{8,4},{12,16},{16,12},{20,24},{24,20},{28,32},{32,28},{36,40... | collective-permute-start | bytes 1179656 | tf_op jit(solution)/shard_map/ppermute | solution.py:308
  9.1 6.8 %collective-permute-start.1 = (bf16[768,256]{1,0:T(8,128)(2,1)}, bf16[768,256]{1,0:T(8,128)(2,1)S(1)}, u32[]{:S(2)}, u32[]{:S(2)}) collective-permute-start(bf16[768,256]{1,0:T(8,128)(2,1)} %get-tuple-element.22), channel_id=1, source_target_pairs={{0,4},{4,0},{8,12},{12,8},{16,20},{20,16},{24,28},{28,24},{32,36},... | collective-permute-start | bytes 1179656 | tf_op jit(solution)/shard_map/ppermute | solution.py:313
  21.2 11.5 %collective-permute-start.2 = (bf16[272,768]{1,0:T(8,128)(2,1)S(1)}, bf16[272,768]{1,0:T(8,128)(2,1)S(1)}, u32[]{:S(2)}, u32[]{:S(2)}) collective-permute-start(bf16[272,768]{1,0:T(8,128)(2,1)S(1)} %get-tuple-element.28), channel_id=1, source_target_pairs={{4,8},{8,4},{12,16},{16,12},{20,24},{24,20},{28,32},{32,28},{36,40... | collective-permute-start | bytes 1253384 | tf_op jit(solution)/shard_map/ppermute | solution.py:308
  25.8 6.9 %collective-permute-start.3 = (bf16[272,768]{1,0:T(8,128)(2,1)S(1)}, bf16[272,768]{1,0:T(8,128)(2,1)S(1)}, u32[]{:S(2)}, u32[]{:S(2)}) collective-permute-start(bf16[272,768]{1,0:T(8,128)(2,1)S(1)} %get-tuple-element.29), channel_id=1, source_target_pairs={{0,4},{4,0},{8,12},{12,8},{16,20},{20,16},{24,28},{28,24},{32,36},... | collective-permute-start | bytes 1253384 | tf_op jit(solution)/shard_map/ppermute | solution.py:313
  25.8 6.8 %copy-start = (s32[4,1]{0,1:T(1,128)S(1)}, s32[4,1]{0,1:T(1,128)}, u32[]{:S(2)}) copy-start(s32[4,1]{0,1:T(1,128)} %param.19) | copy-start | bytes 52
  33.6 12.6 %collective-permute-start.4 = (bf16[64,2688]{1,0:T(8,128)(2,1)S(1)}, bf16[64,2688]{1,0:T(8,128)(2,1)S(1)}, u32[]{:S(2)}, u32[]{:S(2)}) collective-permute-start(bf16[64,2688]{1,0:T(8,128)(2,1)S(1)} %get-tuple-element.35), channel_id=1, source_target_pairs={{0,2},{1,3},{2,0},{3,1},{4,6},{5,7},{6,4},{7,5},{8,10},{9,11},{10,... | collective-permute-start | bytes 1032200 | tf_op jit(solution)/shard_map/ppermute | solution.py:401
  36.7 14.5 %collective-permute-start.5 = (bf16[64,2688]{1,0:T(8,128)(2,1)S(1)}, bf16[64,2688]{1,0:T(8,128)(2,1)S(1)}, u32[]{:S(2)}, u32[]{:S(2)}) collective-permute-start(bf16[64,2688]{1,0:T(8,128)(2,1)S(1)} %get-tuple-element.36), channel_id=1, source_target_pairs={{0,1},{1,2},{2,3},{3,0},{4,5},{5,6},{6,7},{7,4},{8,9},{9,10},{10,1... | collective-permute-start | bytes 1032200 | tf_op jit(solution)/shard_map/ppermute | solution.py:401
  37.3 14.0 %collective-permute-start.6 = (bf16[64,2688]{1,0:T(8,128)(2,1)S(1)}, bf16[64,2688]{1,0:T(8,128)(2,1)S(1)}, u32[]{:S(2)}, u32[]{:S(2)}) collective-permute-start(bf16[64,2688]{1,0:T(8,128)(2,1)S(1)} %get-tuple-element.37), channel_id=1, source_target_pairs={{0,3},{1,0},{2,1},{3,2},{4,7},{5,4},{6,5},{7,6},{8,11},{9,8},{10,9... | collective-permute-start | bytes 1032200 | tf_op jit(solution)/shard_map/ppermute | solution.py:401
